TPU v7x, 32 devices: a whole 2x2x4 slice. The times are simulated.
32 devices in a mesh: tm: 32 (over z, y, x, core), tile: 1.
Axes of the slice: x: 2, y: 2, z: 4, core: 2. Of those that a mesh axis runs over, the one named last changes fastest.
Arguments:
- movie_frames: bfloat16 [32, 1024, 1024], P('tm', None, 'tile'), may hold values from -6 to 6
- patch_weight: bfloat16 [64, 128], replicated, may hold values from -0.75 to 0.75
- depth_weight: bfloat16 [3, 3, 3, 128], replicated, may hold values from -4 to 4
- point_weight: bfloat16 [3, 128, 128], replicated, may hold values from -0.5 to 0.5
- observe_weight: bfloat16 [16, 16, 128, 256], P('tile'), may hold values from -0.03125 to 0.03125
- input_map: float32 [256, 256], replicated, may hold values from -0.375 to 0.375
- mode_decay: float32 [128], replicated, may hold values from 0.86 to 1, as said below
- mode_angle: float32 [128], replicated, may hold values from -0.1 to 0.1
- smooth_decay: float32 [128], replicated, may hold values from 0.86 to 1, as said below
- smooth_angle: float32 [128], replicated, may hold values from -0.1 to 0.1
- readout: float32 [256, 256], replicated, may hold values from -0.375 to 0.375
Outputs:
- latent: float32 [32, 256], P('tm', 'tile')
Inputs may be any that keep to these rules, and one draw needn't show every extreme that they name: `mode_decay`: every mode's magnitude per frame lies strictly below one. `smooth_decay`: every mode's gain magnitude per frame lies strictly below one.
All inputs are finite; a program needn't handle non-finite values.
Results may differ from a plain program's by a relative error of at most 0.00075.
Values may be sent and summed in bfloat16 or wider, within the bound.
A program may use at most 128 MiB of HBM per device.

v0:
```python
import jax
import jax.numpy as jnp
from jax import lax
from jax.sharding import PartitionSpec as P

PATCH = 8
POOL = 8
LAYERS = 3


def passed_along(x, axis, by):
    length = lax.axis_size(axis)
    pairs = [(i, i + by) for i in range(length) if 0 <= i + by < length]
    return lax.ppermute(x, axis, pairs)


def with_halo(x, sides, width):
    for axis, dim in sides:
        size, length = (lax.axis_size(axis), x.shape[dim])
        up = [(i, (i + 1) % size) for i in range(size - 1)]
        down = [(j, i) for i, j in up]
        last = lax.slice_in_dim(x, length - width, length, axis=dim)
        initial = lax.slice_in_dim(x, 0, width, axis=dim)
        before = lax.ppermute(last, axis, up)
        after = lax.ppermute(initial, axis, down)
        x = jnp.concatenate([before, x, after], axis=dim)
    return x


def rotate(state, magnitude, cosine, sine):
    real_part = state[..., 0]
    imag_part = state[..., 1]
    return jnp.stack(
        [
            magnitude * (cosine * real_part - sine * imag_part),
            magnitude * (sine * real_part + cosine * imag_part),
        ],
        axis=-1,
    )


def run_chain(inputs, magnitude, cosine, sine, initial, backward):

    def advance(state, element):
        updated = rotate(state, magnitude, cosine, sine) + element
        return (updated, updated)

    final_state, states = lax.scan(advance, initial, inputs, reverse=backward)
    return states


def block_power(magnitude, angles, frame_count):
    scaled = magnitude**frame_count
    return (scaled * jnp.cos(frame_count * angles), scaled * jnp.sin(frame_count * angles))


def forward_entry(summary, magnitude, angles, frame_count):
    time_count = lax.axis_size("tm")
    power_real, power_imag = block_power(magnitude, angles, frame_count)
    incoming = passed_along(summary, "tm", 1)
    stride = 1
    while stride < time_count:
        arrived = passed_along(incoming, "tm", stride)
        incoming = incoming + rotate(arrived, 1.0, power_real, power_imag)
        power_real, power_imag = (
            power_real * power_real - power_imag * power_imag,
            2.0 * power_real * power_imag,
        )
        stride = stride * 2
    return incoming


def backward_entry(summary, magnitude, angles, frame_count):
    time_count = lax.axis_size("tm")
    power_real, power_imag = block_power(magnitude, angles, frame_count)
    incoming = passed_along(summary, "tm", -1)
    stride = 1
    while stride < time_count:
        arrived = passed_along(incoming, "tm", -stride)
        incoming = incoming + rotate(arrived, 1.0, power_real, power_imag)
        power_real, power_imag = (
            power_real * power_real - power_imag * power_imag,
            2.0 * power_real * power_imag,
        )
        stride = stride * 2
    return incoming


def block_chain(inputs, magnitude, angles, backward, direction):
    frame_count = inputs.shape[0]
    cosine = jnp.cos(angles)
    sine = jnp.sin(angles)
    zero_state = jnp.zeros(inputs.shape[1:], jnp.float32)
    local_states = run_chain(inputs, magnitude, cosine, sine, zero_state, backward)
    if direction == "forward":
        incoming = forward_entry(local_states[-1], magnitude, angles, frame_count)
    else:
        incoming = backward_entry(local_states[0], magnitude, angles, frame_count)
    return run_chain(inputs, magnitude, cosine, sine, incoming, backward)


def embed(frames, patch_weight):
    frame_count, height, width = frames.shape
    grid_rows = height // PATCH
    grid_cols = width // PATCH
    patches = (
        frames.reshape(frame_count, grid_rows, PATCH, grid_cols, PATCH)
        .transpose(0, 1, 3, 2, 4)
        .reshape(frame_count, grid_rows, grid_cols, PATCH * PATCH)
    )
    return jax.nn.gelu(jnp.dot(patches, patch_weight, preferred_element_type=jnp.float32)).astype(
        jnp.bfloat16
    )


def conv_layer(hidden, padded, depth_weight, point_weight, layer_index):
    grid_rows = hidden.shape[1]
    grid_cols = hidden.shape[2]
    summed = jnp.zeros(hidden.shape, jnp.float32)
    for row_shift in range(3):
        for col_shift in range(3):
            kernel = depth_weight[layer_index, row_shift, col_shift].astype(jnp.float32)
            summed = (
                summed
                + padded[
                    :, row_shift : row_shift + grid_rows, col_shift : col_shift + grid_cols
                ].astype(jnp.float32)
                * kernel
            )
    depthwise = summed.astype(jnp.bfloat16)
    branch = jax.nn.gelu(
        jnp.dot(depthwise, point_weight[layer_index], preferred_element_type=jnp.float32)
    )
    return (hidden.astype(jnp.float32) + branch).astype(jnp.bfloat16)


def shards(
    movie_frames,
    patch_weight,
    depth_weight,
    point_weight,
    observe_weight,
    input_map,
    mode_decay,
    mode_angle,
    smooth_decay,
    smooth_angle,
    readout,
):
    frame_count, height, width = movie_frames.shape
    grid_rows = height // PATCH
    grid_cols = width // PATCH
    channels = patch_weight.shape[1]
    tile_count = lax.axis_size("tile")
    tile_index = lax.axis_index("tile")
    hidden = embed(movie_frames, patch_weight)
    for layer_index in range(LAYERS):
        widened = with_halo(hidden, (("tile", 2),), 1)
        padded = jnp.pad(widened, ((0, 0), (1, 1), (0, 0), (0, 0)))
        hidden = conv_layer(hidden, padded, depth_weight, point_weight, layer_index)
    pooled = jnp.mean(
        hidden.astype(jnp.float32).reshape(
            frame_count, grid_rows // POOL, POOL, grid_cols // POOL, POOL, channels
        ),
        axis=(2, 4),
    ).astype(jnp.bfloat16)
    features = pooled.transpose(0, 2, 1, 3).reshape(frame_count, -1)
    partial_value = jnp.dot(
        features,
        observe_weight.reshape(-1, observe_weight.shape[-1]),
        preferred_element_type=jnp.float32,
    )
    latent_share = readout.shape[0] // tile_count
    observed = lax.psum(partial_value, "tile")
    drive = jnp.dot(observed, input_map.T, precision=lax.Precision.HIGHEST)
    magnitude, angles = (mode_decay, mode_angle)
    back_magnitude, back_angles = (smooth_decay, smooth_angle)
    mode_count = magnitude.shape[0]
    drive = (
        drive.reshape(frame_count, mode_count, 2) * jnp.sqrt(1.0 - magnitude * magnitude)[:, None]
    )
    filtered = block_chain(drive, magnitude, angles, False, "forward")
    weighted = filtered * jnp.sqrt(1.0 - back_magnitude * back_magnitude)[:, None]
    smoothed = block_chain(weighted, back_magnitude, back_angles, True, "backward")
    smoothed_flat = smoothed.reshape(frame_count, 2 * mode_count)
    latent_rows = lax.dynamic_slice_in_dim(readout, tile_index * latent_share, latent_share, 0)
    return jnp.dot(smoothed_flat, latent_rows.T, precision=lax.Precision.HIGHEST)


def solution(mesh):
    placed = (
        P("tm", None, "tile"),
        P(),
        P(),
        P(),
        P("tile", None, None, None),
        P(),
        P(),
        P(),
        P(),
        P(),
        P(),
    )
    return jax.shard_map(
        shards, mesh=mesh, in_specs=placed, out_specs=P("tm", "tile"), check_vma=False
    )
```

profile of v0, /device:TPU:0, one launch (start us, length us, event | category | flops | bytes accessed | tf_op | source)
XLA Modules:
  0.0 229.5 jit_solution(14086372378552696291)
XLA Ops:
  0.0 42.1 %reshape.229 = bf16[1,128,8,128,8]{4,3,2,1,0:T(8,128)(2,1)} reshape(bf16[1,1024,1024]{2,1,0:T(8,128)(2,1)} %param.11) | data formatting | bytes 4194304 | tf_op jit(solution)/shard_map/reshape | solution.py:107
  42.1 24.0 %copy.16 = bf16[1,128,128,8,8]{2,4,3,1,0:T(8,128)(2,1)S(1)} copy(bf16[1,128,128,8,8]{4,2,3,1,0:T(8,128)(2,1)} %bitcast.479) | data formatting | bytes 4194304 | tf_op jit(solution)/shard_map/transpose | solution.py:108
  66.1 3.2 %fusion.32 = bf16[128,128,128]{2,1,0:T(8,128)(2,1)S(1)} fusion(bf16[1,128,128,8,8]{2,4,3,1,0:T(8,128)(2,1)S(1)} %copy.16, bf16[64,128]{1,0:T(8,128)(2,1)S(1)} %copy-done.7), kind=kOutput, calls=%fused_computation.44 | convolution fusion | flops 287309824 | bytes 6307840 | tf_op jit(solution)/shard_map/dot_general | solution.py:111
  70.9 5.2 %select_maximum_fusion.4 = bf16[1,130,130,128]{3,2,1,0:T(8,128)(2,1)S(1)} fusion(bf16[1,128,1,128]{3,2,1,0:T(2,128)(2,1)S(1)} %collective-permute-done.1, bf16[1,128,128,128]{3,2,1,0:T(8,128)(2,1)S(1)} %bitcast.487, bf16[1,128,1,128]{3,2,1,0:T(2,128)(2,1)S(1)} %collective-permute-done), kind=kLoop, calls=%fused_computation.71 | loop fusion | flops 25958400 | bytes 8586240 | tf_op jit(solution)/shard_map/concatenate | solution.py:26
  76.1 13.4 %fusion.8 = bf16[128,128,128]{2,1,0:T(8,128)(2,1)S(1)} fusion(bf16[128,128,128]{2,1,0:T(8,128)(2,1)S(1)} %fusion.32, f32[128]{0:T(128)S(1)} %get-tuple-element.135, bf16[1,130,130,128]{3,2,1,0:T(8,128)(2,1)S(1)} %select_maximum_fusion.4, f32[128]{0:T(128)S(1)} %get-tuple-element.136, f32[128]{0:T(128)S(1)} %get-tuple-element.137, ...), kind=kOutput, calls=%fused_computation.20 | convolution fusion | flops 629145600 | bytes 42111488 | tf_op jit(solution)/shard_map/dot_general | solution.py:132
  91.2 5.2 %select_maximum_fusion.2 = bf16[1,130,130,128]{3,2,1,0:T(8,128)(2,1)S(1)} fusion(bf16[1,128,1,128]{3,2,1,0:T(2,128)(2,1)S(1)} %collective-permute-done.3, bf16[1,128,128,128]{3,2,1,0:T(8,128)(2,1)S(1)} %bitcast.490, bf16[1,128,1,128]{3,2,1,0:T(2,128)(2,1)S(1)} %collective-permute-done.2), kind=kLoop, calls=%fused_computation.69 | loop fusion | flops 25958400 | bytes 8586240 | tf_op jit(solution)/shard_map/concatenate | solution.py:26
  96.4 13.4 %fusion.16 = bf16[128,128,128]{2,1,0:T(8,128)(2,1)S(1)} fusion(bf16[128,128,128]{2,1,0:T(8,128)(2,1)S(1)} %fusion.8, f32[128]{0:T(128)S(1)} %get-tuple-element.126, bf16[1,130,130,128]{3,2,1,0:T(8,128)(2,1)S(1)} %select_maximum_fusion.2, f32[128]{0:T(128)S(1)} %get-tuple-element.127, f32[128]{0:T(128)S(1)} %get-tuple-element.128, ...), kind=kOutput, calls=%fused_computation.28 | convolution fusion | flops 629145600 | bytes 42111488 | tf_op jit(solution)/shard_map/dot_general | solution.py:132
  109.7 2.0 copy-done.1
  113.4 8.1 %select_maximum_fusion = bf16[1,130,130,128]{3,2,1,0:T(8,128)(2,1)} fusion(bf16[1,128,1,128]{3,2,1,0:T(2,128)(2,1)S(1)} %collective-permute-done.5, bf16[1,128,128,128]{3,2,1,0:T(8,128)(2,1)} %bitcast.484, bf16[1,128,1,128]{3,2,1,0:T(2,128)(2,1)S(1)} %collective-permute-done.4), kind=kLoop, calls=%fused_computation.67 | loop fusion | flops 25958400 | bytes 8586240 | tf_op jit(solution)/shard_map/concatenate | solution.py:26
  121.5 28.7 %fusion.24 = bf16[128,128,128]{2,1,0:T(8,128)(2,1)} fusion(bf16[128,128,128]{2,1,0:T(8,128)(2,1)} %copy-done.1, f32[128]{0:T(128)S(1)} %get-tuple-element.145, bf16[1,130,130,128]{3,2,1,0:T(8,128)(2,1)} %select_maximum_fusion, f32[128]{0:T(128)S(1)} %get-tuple-element.138, f32[128]{0:T(128)S(1)} %get-tuple-element.120, f32[128]{0:T(128)S(1)} %get-tuple-element.121, ...), kind=kOutput, calls=%fused_computation.36 | convolution fusion | flops 629145600 | bytes 42111488 | tf_op jit(solution)/shard_map/dot_general | solution.py:132
  150.2 3.1 %convert_reduce_fusion = f32[16,16,128]{2,1,0:T(8,128)S(1)} fusion(bf16[16,8,16,8,128]{4,3,2,1,0:T(8,128)(2,1)} %bitcast.492), kind=kLoop, calls=%fused_computation.66 | loop fusion | flops 4161536 | bytes 4325376 | tf_op jit(solution)/shard_map/reduce_sum | solution.py:161
  153.5 2.3 fusion.139
  156.1 2.4 %collective-permute-start.6 = (f32[128,2]{0,1:T(2,128)S(1)}, f32[128,2]{0,1:T(2,128)S(1)}, u32[]{:S(2)}, u32[]{:S(2)}) collective-permute-start(f32[128,2]{0,1:T(2,128)S(1)} %maximum_add_fusion.1), channel_id=1, source_target_pairs={{0,1},{1,2},{2,3},{3,4},{4,5},{5,6},{6,7},{7,8},{8,9},{9,10},{10,1... | collective-permute-start | bytes 3080 | tf_op jit(solution)/shard_map/ppermute | solution.py:14
  159.2 4.4 %collective-permute-start.7 = (f32[128,2]{0,1:T(2,128)S(1)}, f32[128,2]{0,1:T(2,128)S(1)}, u32[]{:S(2)}, u32[]{:S(2)}) collective-permute-start(f32[128,2]{0,1:T(2,128)S(1)} %collective-permute-done.6), channel_id=1, source_target_pairs={{0,1},{1,2},{2,3},{3,4},{4,5},{5,6},{6,7},{7,8},{8,9},{9,10},{10,1... | collective-permute-start | bytes 3080 | tf_op jit(solution)/shard_map/ppermute | solution.py:14
  164.5 6.2 %collective-permute-start.8 = (f32[128,2]{0,1:T(2,128)S(1)}, f32[128,2]{0,1:T(2,128)S(1)}, u32[]{:S(2)}, u32[]{:S(2)}) collective-permute-start(f32[128,2]{0,1:T(2,128)S(1)} %maximum_add_fusion.2), channel_id=1, source_target_pairs={{0,2},{1,3},{2,4},{3,5},{4,6},{5,7},{6,8},{7,9},{8,10},{9,11},{10,... | collective-permute-start | bytes 3080 | tf_op jit(solution)/shard_map/ppermute | solution.py:14
  172.0 6.9 %collective-permute-start.9 = (f32[128,2]{0,1:T(2,128)S(1)}, f32[128,2]{0,1:T(2,128)S(1)}, u32[]{:S(2)}, u32[]{:S(2)}) collective-permute-start(f32[128,2]{0,1:T(2,128)S(1)} %maximum_add_fusion.3), channel_id=1, source_target_pairs={{0,4},{1,5},{2,6},{3,7},{4,8},{5,9},{6,10},{7,11},{8,12},{9,13},{1... | collective-permute-start | bytes 3080 | tf_op jit(solution)/shard_map/ppermute | solution.py:14
  180.3 7.8 %collective-permute-start.10 = (f32[128,2]{0,1:T(2,128)S(1)}, f32[128,2]{0,1:T(2,128)S(1)}, u32[]{:S(2)}, u32[]{:S(2)}) collective-permute-start(f32[128,2]{0,1:T(2,128)S(1)} %maximum_add_fusion.4), channel_id=1, source_target_pairs={{0,8},{1,9},{2,10},{3,11},{4,12},{5,13},{6,14},{7,15},{8,16},{9,17... | collective-permute-start | bytes 3080 | tf_op jit(solution)/shard_map/ppermute | solution.py:14
  189.4 5.2 %collective-permute-start.11 = (f32[128,2]{0,1:T(2,128)S(1)}, f32[128,2]{0,1:T(2,128)S(1)}, u32[]{:S(2)}, u32[]{:S(2)}) collective-permute-start(f32[128,2]{0,1:T(2,128)S(1)} %maximum_add_fusion.5), channel_id=1, source_target_pairs={{0,16},{1,17},{2,18},{3,19},{4,20},{5,21},{6,22},{7,23},{8,24},{9,... | collective-permute-start | bytes 3080 | tf_op jit(solution)/shard_map/ppermute | solution.py:14
  197.2 1.7 collective-permute-done.12
  200.3 1.7 collective-permute-done.13
  203.3 4.2 %collective-permute-done.14 = f32[128,2]{0,1:T(2,128)S(1)} collective-permute-done((f32[128,2]{0,1:T(2,128)S(1)}, f32[128,2]{0,1:T(2,128)S(1)}, u32[]{:S(2)}, u32[]{:S(2)}) %collective-permute-start.14) | collective-permute-done | bytes 1056 | tf_op jit(solution)/shard_map/ppermute | solution.py:14
  208.8 4.9 %collective-permute-done.15 = f32[128,2]{0,1:T(2,128)S(1)} collective-permute-done((f32[128,2]{0,1:T(2,128)S(1)}, f32[128,2]{0,1:T(2,128)S(1)}, u32[]{:S(2)}, u32[]{:S(2)}) %collective-permute-start.15) | collective-permute-done | bytes 1056 | tf_op jit(solution)/shard_map/ppermute | solution.py:14
  215.1 6.8 %collective-permute-done.16 = f32[128,2]{0,1:T(2,128)S(1)} collective-permute-done((f32[128,2]{0,1:T(2,128)S(1)}, f32[128,2]{0,1:T(2,128)S(1)}, u32[]{:S(2)}, u32[]{:S(2)}) %collective-permute-start.16) | collective-permute-done | bytes 1056 | tf_op jit(solution)/shard_map/ppermute | solution.py:14
  223.2 5.1 %collective-permute-done.17 = f32[128,2]{0,1:T(2,128)S(1)} collective-permute-done((f32[128,2]{0,1:T(2,128)S(1)}, f32[128,2]{0,1:T(2,128)S(1)}, u32[]{:S(2)}, u32[]{:S(2)}) %collective-permute-start.17) | collective-permute-done | bytes 1056 | tf_op jit(solution)/shard_map/ppermute | solution.py:14
  (102 shorter events, 21.1 us)
Async XLA Ops:
  0.0 228.6 %copy-start = (f32[256,256]{1,0:T(8,128)S(1)}, f32[256,256]{1,0:T(8,128)}, u32[]{:S(2)}) copy-start(f32[256,256]{1,0:T(8,128)} %param.21) | copy-start | bytes 786436
  42.1 24.0 %copy-start.7 = (bf16[64,128]{1,0:T(8,128)(2,1)S(1)}, bf16[64,128]{1,0:T(8,128)(2,1)}, u32[]{:S(2)}) copy-start(bf16[64,128]{1,0:T(8,128)(2,1)} %param.12) | copy-start | bytes 49156
  69.4 1.4 collective-permute-start
  70.1 0.8 collective-permute-start.1
  89.6 1.6 collective-permute-start.2
  90.2 0.9 collective-permute-start.3
  111.9 1.5 collective-permute-start.4
  112.5 0.9 collective-permute-start.5
  113.4 40.0 %slice-start = ((s8[16777216]{0:T(1024)(128)(4,1)}), s8[4194304]{0:T(1024)(128)(4,1)S(1)}, s32[]{:S(2)}) async-start(s8[16777216]{0:T(1024)(128)(4,1)} %bitcast.480), calls=%async_computation | async-start | bytes 8388608
  121.5 32.0 %slice-start.1 = ((s8[16777216]{0:T(1024)(128)(4,1)}), s8[4194304]{0:T(1024)(128)(4,1)S(1)}, s32[]{:S(2)}) async-start(s8[16777216]{0:T(1024)(128)(4,1)} %bitcast.480), calls=%async_computation.1 | async-start | bytes 8388608
  121.5 32.0 %slice-start.2 = ((s8[16777216]{0:T(1024)(128)(4,1)}), s8[4194304]{0:T(1024)(128)(4,1)S(1)}, s32[]{:S(2)}) async-start(s8[16777216]{0:T(1024)(128)(4,1)} %bitcast.480), calls=%async_computation.2 | async-start | bytes 8388608
  121.5 32.0 %slice-start.3 = ((s8[16777216]{0:T(1024)(128)(4,1)}), s8[4194304]{0:T(1024)(128)(4,1)S(1)}, s32[]{:S(2)}) async-start(s8[16777216]{0:T(1024)(128)(4,1)} %bitcast.480), calls=%async_computation.3 | async-start | bytes 8388608
  156.1 3.2 %collective-permute-start.6 = (f32[128,2]{0,1:T(2,128)S(1)}, f32[128,2]{0,1:T(2,128)S(1)}, u32[]{:S(2)}, u32[]{:S(2)}) collective-permute-start(f32[128,2]{0,1:T(2,128)S(1)} %maximum_add_fusion.1), channel_id=1, source_target_pairs={{0,1},{1,2},{2,3},{3,4},{4,5},{5,6},{6,7},{7,8},{8,9},{9,10},{10,1... | collective-permute-start | bytes 3080 | tf_op jit(solution)/shard_map/ppermute | solution.py:14
  159.2 5.2 %collective-permute-start.7 = (f32[128,2]{0,1:T(2,128)S(1)}, f32[128,2]{0,1:T(2,128)S(1)}, u32[]{:S(2)}, u32[]{:S(2)}) collective-permute-start(f32[128,2]{0,1:T(2,128)S(1)} %collective-permute-done.6), channel_id=1, source_target_pairs={{0,1},{1,2},{2,3},{3,4},{4,5},{5,6},{6,7},{7,8},{8,9},{9,10},{10,1... | collective-permute-start | bytes 3080 | tf_op jit(solution)/shard_map/ppermute | solution.py:14
  164.5 7.5 %collective-permute-start.8 = (f32[128,2]{0,1:T(2,128)S(1)}, f32[128,2]{0,1:T(2,128)S(1)}, u32[]{:S(2)}, u32[]{:S(2)}) collective-permute-start(f32[128,2]{0,1:T(2,128)S(1)} %maximum_add_fusion.2), channel_id=1, source_target_pairs={{0,2},{1,3},{2,4},{3,5},{4,6},{5,7},{6,8},{7,9},{8,10},{9,11},{10,... | collective-permute-start | bytes 3080 | tf_op jit(solution)/shard_map/ppermute | solution.py:14
  172.0 8.2 %collective-permute-start.9 = (f32[128,2]{0,1:T(2,128)S(1)}, f32[128,2]{0,1:T(2,128)S(1)}, u32[]{:S(2)}, u32[]{:S(2)}) collective-permute-start(f32[128,2]{0,1:T(2,128)S(1)} %maximum_add_fusion.3), channel_id=1, source_target_pairs={{0,4},{1,5},{2,6},{3,7},{4,8},{5,9},{6,10},{7,11},{8,12},{9,13},{1... | collective-permute-start | bytes 3080 | tf_op jit(solution)/shard_map/ppermute | solution.py:14
  180.3 9.1 %collective-permute-start.10 = (f32[128,2]{0,1:T(2,128)S(1)}, f32[128,2]{0,1:T(2,128)S(1)}, u32[]{:S(2)}, u32[]{:S(2)}) collective-permute-start(f32[128,2]{0,1:T(2,128)S(1)} %maximum_add_fusion.4), channel_id=1, source_target_pairs={{0,8},{1,9},{2,10},{3,11},{4,12},{5,13},{6,14},{7,15},{8,16},{9,17... | collective-permute-start | bytes 3080 | tf_op jit(solution)/shard_map/ppermute | solution.py:14
  189.4 6.5 %collective-permute-start.11 = (f32[128,2]{0,1:T(2,128)S(1)}, f32[128,2]{0,1:T(2,128)S(1)}, u32[]{:S(2)}, u32[]{:S(2)}) collective-permute-start(f32[128,2]{0,1:T(2,128)S(1)} %maximum_add_fusion.5), channel_id=1, source_target_pairs={{0,16},{1,17},{2,18},{3,19},{4,20},{5,21},{6,22},{7,23},{8,24},{9,... | collective-permute-start | bytes 3080 | tf_op jit(solution)/shard_map/ppermute | solution.py:14
  195.9 3.0 %collective-permute-start.12 = (f32[128,2]{0,1:T(2,128)S(1)}, f32[128,2]{0,1:T(2,128)S(1)}, u32[]{:S(2)}, u32[]{:S(2)}) collective-permute-start(f32[128,2]{0,1:T(2,128)S(1)} %maximum_add_fusion), channel_id=1, source_target_pairs={{1,0},{2,1},{3,2},{4,3},{5,4},{6,5},{7,6},{8,7},{9,8},{10,9},{11,1... | collective-permute-start | bytes 3080 | tf_op jit(solution)/shard_map/ppermute | solution.py:14
  199.0 3.0 %collective-permute-start.13 = (f32[128,2]{0,1:T(2,128)S(1)}, f32[128,2]{0,1:T(2,128)S(1)}, u32[]{:S(2)}, u32[]{:S(2)}) collective-permute-start(f32[128,2]{0,1:T(2,128)S(1)} %collective-permute-done.12), channel_id=1, source_target_pairs={{1,0},{2,1},{3,2},{4,3},{5,4},{6,5},{7,6},{8,7},{9,8},{10,9},{11,1... | collective-permute-start | bytes 3080 | tf_op jit(solution)/shard_map/ppermute | solution.py:14
  202.0 5.5 %collective-permute-start.14 = (f32[128,2]{0,1:T(2,128)S(1)}, f32[128,2]{0,1:T(2,128)S(1)}, u32[]{:S(2)}, u32[]{:S(2)}) collective-permute-start(f32[128,2]{0,1:T(2,128)S(1)} %maximum_add_fusion.8), channel_id=1, source_target_pairs={{2,0},{3,1},{4,2},{5,3},{6,4},{7,5},{8,6},{9,7},{10,8},{11,9},{12,... | collective-permute-start | bytes 3080 | tf_op jit(solution)/shard_map/ppermute | solution.py:14
  207.5 6.2 %collective-permute-start.15 = (f32[128,2]{0,1:T(2,128)S(1)}, f32[128,2]{0,1:T(2,128)S(1)}, u32[]{:S(2)}, u32[]{:S(2)}) collective-permute-start(f32[128,2]{0,1:T(2,128)S(1)} %maximum_add_fusion.9), channel_id=1, source_target_pairs={{4,0},{5,1},{6,2},{7,3},{8,4},{9,5},{10,6},{11,7},{12,8},{13,9},{1... | collective-permute-start | bytes 3080 | tf_op jit(solution)/shard_map/ppermute | solution.py:14
  213.8 8.1 %collective-permute-start.16 = (f32[128,2]{0,1:T(2,128)S(1)}, f32[128,2]{0,1:T(2,128)S(1)}, u32[]{:S(2)}, u32[]{:S(2)}) collective-permute-start(f32[128,2]{0,1:T(2,128)S(1)} %maximum_add_fusion.10), channel_id=1, source_target_pairs={{8,0},{9,1},{10,2},{11,3},{12,4},{13,5},{14,6},{15,7},{16,8},{17,9... | collective-permute-start | bytes 3080 | tf_op jit(solution)/shard_map/ppermute | solution.py:14
  221.9 6.4 %collective-permute-start.17 = (f32[128,2]{0,1:T(2,128)S(1)}, f32[128,2]{0,1:T(2,128)S(1)}, u32[]{:S(2)}, u32[]{:S(2)}) collective-permute-start(f32[128,2]{0,1:T(2,128)S(1)} %maximum_add_fusion.11), channel_id=1, source_target_pairs={{16,0},{17,1},{18,2},{19,3},{20,4},{21,5},{22,6},{23,7},{24,8},{25... | collective-permute-start | bytes 3080 | tf_op jit(solution)/shard_map/ppermute | solution.py:14
  (8 other events, 83.8 us)
where the time goes:
time: 231 us; the launch traced here: 230 us
  local copies, waits for them, and re-layouts  69.1 us (30%)
  matrix products  61.8 us (27%)
  starting transfers between devices  44.8 us (19%)
  waiting for transfers between devices  31.2 us (14%)
  other arithmetic  22 us (10%)
    dot_general x3, matrix products, conv_layer(): jnp.dot(depthwise, point_weight[layer_index], preferred_element_type=jnp....  55.5 us
    reshape x1, local copies, waits for them, and re-layouts, embed(): frames.reshape(frame_count, grid_rows, PATCH, grid_cols, PATCH)  42.1 us
    ppermute x12, starting transfers between devices, passed_along(): return lax.ppermute(x, axis, pairs)  40.7 us
    ppermute x12, waiting for transfers between devices, passed_along(): return lax.ppermute(x, axis, pairs)  31.2 us
    transpose x1, local copies, waits for them, and re-layouts, embed(): patches = frames.reshape(frame_count, grid_rows, PATCH, grid_cols, PATCH)...  24 us
    concatenate x3, other arithmetic, with_halo(): x = jnp.concatenate([before, x, after], axis=dim)  18.4 us
  transfers between devices with their start and end apart: 18, of which 12 were waited for; matrix products, arithmetic and copies ran while one was open for 0% of the time, Pallas kernels for 0%

commit v1 on v0

v1 whole, which is shorter than its diff:
```python
import functools
import math

import jax
import jax.numpy as jnp
from jax import lax
from jax.experimental import pallas as pl
from jax.experimental.pallas import tpu as pltpu
from jax.sharding import PartitionSpec as P

PATCH = 8
POOL = 8
LAYERS = 3


def with_halo(x, sides, width):
    for axis, dim in sides:
        size, length = (lax.axis_size(axis), x.shape[dim])
        up = [(i, (i + 1) % size) for i in range(size - 1)]
        down = [(j, i) for i, j in up]
        last = lax.slice_in_dim(x, length - width, length, axis=dim)
        initial = lax.slice_in_dim(x, 0, width, axis=dim)
        before = lax.ppermute(last, axis, up)
        after = lax.ppermute(initial, axis, down)
        x = jnp.concatenate([before, x, after], axis=dim)
    return x


def embed(frames, patch_weight):
    frame_count, height, width = frames.shape
    grid_rows = height // PATCH
    grid_cols = width // PATCH
    patches = (
        frames.reshape(frame_count, grid_rows, PATCH, grid_cols, PATCH)
        .transpose(0, 1, 3, 2, 4)
        .reshape(frame_count, grid_rows, grid_cols, PATCH * PATCH)
    )
    return jax.nn.gelu(jnp.dot(patches, patch_weight, preferred_element_type=jnp.float32)).astype(
        jnp.bfloat16
    )


def conv_layer(hidden, padded, depth_weight, point_weight, layer_index):
    grid_rows = hidden.shape[1]
    grid_cols = hidden.shape[2]
    summed = jnp.zeros(hidden.shape, jnp.float32)
    for row_shift in range(3):
        for col_shift in range(3):
            kernel = depth_weight[layer_index, row_shift, col_shift].astype(jnp.float32)
            summed = (
                summed
                + padded[
                    :, row_shift : row_shift + grid_rows, col_shift : col_shift + grid_cols
                ].astype(jnp.float32)
                * kernel
            )
    depthwise = summed.astype(jnp.bfloat16)
    branch = jax.nn.gelu(
        jnp.dot(depthwise, point_weight[layer_index], preferred_element_type=jnp.float32)
    )
    return (hidden.astype(jnp.float32) + branch).astype(jnp.bfloat16)

GELU_LINEAR = 2.0 * math.sqrt(2.0 / math.pi)
GELU_CUBIC = 4.0 * 0.044715 * GELU_LINEAR
EDGE = 8
GROUP = 8
STRIP = 16


def gelu_of_half(half):
    inner = half * (GELU_LINEAR + GELU_CUBIC * (half * half))
    return half + half * jnp.tanh(inner)


def encoder_kernel(
    frame_ref,
    patch_ref,
    depth_ref,
    point_ref,
    observe_ref,
    out_ref,
    cells,
    spread,
    first,
    second,
    mixed,
    depth_rows,
    point_pair,
    observe,
    observe_sem,
):
    height, width = frame_ref.shape
    channels = patch_ref.shape[1]
    rows, cols = height // PATCH, width // PATCH
    lane_groups = width // 128
    group_cols = 128 // PATCH
    pool_cols, pool_rows = cols // POOL, rows // POOL

    def observe_copy(index):
        return pltpu.make_async_copy(
            observe_ref.at[index], observe.at[index], observe_sem.at[index]
        )

    for index in range(pool_cols):
        observe_copy(index).start()

    patch = patch_ref[...].astype(jnp.float32) * 0.5
    blank = jnp.zeros((PATCH, channels), jnp.float32)
    spread[...] = jnp.zeros_like(spread)
    for i in range(PATCH):
        part = patch[i * PATCH : (i + 1) * PATCH]
        block = jnp.concatenate(
            [
                jnp.concatenate([part, blank], axis=1),
                jnp.concatenate([blank, part], axis=1),
            ],
            axis=0,
        ).astype(jnp.bfloat16)
        for n in range(group_cols // 2):
            spread[n, pl.ds(i * 128 + n * 2 * PATCH, 2 * PATCH), :] = block
    square = jnp.zeros((channels, channels), jnp.bfloat16)
    for layer in range(LAYERS):
        point = (point_ref[layer].astype(jnp.float32) * 0.5).astype(jnp.bfloat16)
        point_pair[layer, :channels, :channels] = point
        point_pair[layer, channels:, channels:] = point
        point_pair[layer, :channels, channels:] = square
        point_pair[layer, channels:, :channels] = square
    depth = depth_ref[...].astype(jnp.float32)
    for tap in range(LAYERS * 9):
        depth_rows[tap] = jnp.broadcast_to(depth[tap : tap + 1], (STRIP, channels))

    for ref in (first, second):
        column = jnp.zeros(ref.shape[1:], jnp.float32)
        ref[0] = column
        ref[cols + 1] = column
        edge = jnp.zeros((cols + 2, EDGE, channels), jnp.float32)
        ref[:, :EDGE, :] = edge
        ref[:, EDGE + rows :, :] = edge

    row_block = 256
    row_cells = row_block // PATCH
    to_row = lax.broadcasted_iota(jnp.int32, (row_block, row_block), 0)
    from_row = lax.broadcasted_iota(jnp.int32, (row_block, row_block), 1)
    order = jnp.where(
        (from_row % PATCH == to_row // row_cells) & (from_row // PATCH == to_row % row_cells),
        1.0,
        0.0,
    ).astype(jnp.bfloat16)
    for b in range(height // row_block):
        ordered = jnp.dot(
            order,
            frame_ref[b * row_block : (b + 1) * row_block, :],
            preferred_element_type=jnp.float32,
        ).astype(jnp.bfloat16)
        for g in range(lane_groups):
            for i in range(PATCH):
                cells[
                    g, b * row_cells : (b + 1) * row_cells, i * 128 : (i + 1) * 128
                ] = ordered[i * row_cells : (i + 1) * row_cells, g * 128 : (g + 1) * 128]

    half_groups = max(lane_groups // 2, 1)

    def embed_step(step, carry):
        n = step // (lane_groups // half_groups)
        part = step % (lane_groups // half_groups)
        taken = cells[pl.ds(part * half_groups, half_groups)].reshape(
            half_groups * rows, PATCH * 128
        )
        half = jnp.dot(taken, spread[n], preferred_element_type=jnp.float32)
        for g in range(half_groups):
            value = gelu_of_half(half[g * rows : (g + 1) * rows])
            value = value.astype(jnp.bfloat16).astype(jnp.float32)
            column = (part * half_groups + g) * group_cols + 2 * n + 1
            first[column, EDGE : EDGE + rows, :] = value[:, :channels]
            first[column + 1, EDGE : EDGE + rows, :] = value[:, channels:]
        return carry

    lax.fori_loop(0, (group_cols // 2) * (lane_groups // half_groups), embed_step, 0)

    def layer_branch(layer, source, group):
        start = group * GROUP
        for p in range(GROUP // 2):
            for strip in range(rows // STRIP):
                sums = [None, None]
                for dr in range(3):
                    for cc in range(4):
                        taken = source[
                            start + 2 * p + cc, pl.ds(EDGE - 1 + strip * STRIP + dr, STRIP), :
                        ]
                        for o in range(2):
                            dc = cc - o
                            if 0 <= dc <= 2:
                                term = taken * depth_rows[layer * 9 + dr * 3 + dc]
                                sums[o] = term if sums[o] is None else sums[o] + term
                for o in range(2):
                    mixed[
                        p * rows + strip * STRIP : p * rows + (strip + 1) * STRIP,
                        o * channels : (o + 1) * channels,
                    ] = sums[o].astype(jnp.bfloat16)
        return jnp.dot(mixed[...], point_pair[layer], preferred_element_type=jnp.float32)

    def updated(source, group, half, p, o):
        column = group * GROUP + 2 * p + o + 1
        branch = gelu_of_half(
            half[p * rows : (p + 1) * rows, o * channels : (o + 1) * channels]
        )
        value = source[column, EDGE : EDGE + rows, :] + branch
        return column, value.astype(jnp.bfloat16).astype(jnp.float32)

    def layer_step(layer, source, target, group, carry):
        half = layer_branch(layer, source, group)
        for p in range(GROUP // 2):
            for o in range(2):
                column, value = updated(source, group, half, p, o)
                target[column, EDGE : EDGE + rows, :] = value
        return carry

    def last_step(source, group, total):
        half = layer_branch(LAYERS - 1, source, group)
        summed = jnp.zeros((rows, channels), jnp.float32)
        for p in range(GROUP // 2):
            for o in range(2):
                summed = summed + updated(source, group, half, p, o)[1]
        pooled = jnp.sum(summed.reshape(pool_rows, POOL, channels), axis=1) * (
            1.0 / (POOL * POOL)
        )
        own = lax.broadcasted_iota(jnp.int32, (pool_rows, channels), 0)
        features = jnp.concatenate(
            [jnp.where(own == r, pooled, 0.0) for r in range(pool_rows)], axis=1
        ).astype(jnp.bfloat16)
        observe_copy(group).wait()
        return total + jnp.dot(features, observe[group], preferred_element_type=jnp.float32)

    refs = (first, second)
    for layer in range(LAYERS - 1):
        lax.fori_loop(
            0,
            cols // GROUP,
            functools.partial(layer_step, layer, refs[layer % 2], refs[(layer + 1) % 2]),
            0,
        )
    total = lax.fori_loop(
        0,
        pool_cols,
        functools.partial(last_step, refs[(LAYERS - 1) % 2]),
        jnp.zeros((pool_rows, observe.shape[2]), jnp.float32),
    )
    out_ref[...] = jnp.sum(total, axis=0, keepdims=True)


def encode_whole(frame, patch_weight, depth_weight, point_weight, observe_weight):
    height, width = frame.shape
    channels = patch_weight.shape[1]
    rows, cols = height // PATCH, width // PATCH
    pool_cols, pool_rows, _, components = observe_weight.shape
    observe_weight = observe_weight.reshape(pool_cols, pool_rows * channels, components)
    vmem = pl.BlockSpec(memory_space=pltpu.VMEM)
    padded = (cols + 2, rows + 2 * EDGE, channels)
    return pl.pallas_call(
        encoder_kernel,
        out_shape=jax.ShapeDtypeStruct((1, components), jnp.float32),
        in_specs=[vmem, vmem, vmem, vmem, pl.BlockSpec(memory_space=pl.ANY)],
        out_specs=vmem,
        scratch_shapes=[
            pltpu.VMEM((width // 128, rows, PATCH * 128), jnp.bfloat16),
            pltpu.VMEM((128 // PATCH // 2, PATCH * 128, 2 * channels), jnp.bfloat16),
            pltpu.VMEM(padded, jnp.float32),
            pltpu.VMEM(padded, jnp.float32),
            pltpu.VMEM((GROUP // 2 * rows, 2 * channels), jnp.bfloat16),
            pltpu.VMEM((LAYERS * 9, STRIP, channels), jnp.float32),
            pltpu.VMEM((LAYERS, 2 * channels, 2 * channels), jnp.bfloat16),
            pltpu.VMEM(observe_weight.shape, jnp.bfloat16),
            pltpu.SemaphoreType.DMA((pool_cols,)),
        ],
        compiler_params=pltpu.CompilerParams(vmem_limit_bytes=60 * 1024 * 1024),
        name="encoder",
    )(frame, patch_weight, depth_weight.reshape(-1, channels), point_weight, observe_weight)


def complex_times(a, b):
    return (a[0] * b[0] - a[1] * b[1], a[0] * b[1] + a[1] * b[0])


def filter_kernel(
    count, observed_ref, map_ref, modes_ref, readout_ref, out_ref, gathered, send_sem, recv_sem
):
    me = lax.axis_index("tm")
    barrier = pltpu.get_barrier_semaphore()

    def greet(step, carry):
        pl.semaphore_signal(
            barrier,
            inc=1,
            device_id={"tm": lax.rem(me + step, count)},
            device_id_type=pl.DeviceIdType.MESH,
        )
        return carry

    lax.fori_loop(1, count, greet, 0)

    modes = modes_ref.shape[1]
    state = 2 * modes
    mode = lax.broadcasted_iota(jnp.int32, (modes, state), 0)
    component = lax.broadcasted_iota(jnp.int32, (modes, state), 1)
    repeat = jnp.where(component // 2 == mode, 1.0, 0.0)
    doubled = jnp.dot(
        modes_ref[...],
        repeat,
        precision=lax.Precision.HIGHEST,
        preferred_element_type=jnp.float32,
    )
    decay, angle, back_decay, back_angle = (doubled[k : k + 1] for k in range(4))
    drive = lax.dot_general(
        observed_ref[...],
        map_ref[...],
        (((1,), (1,)), ((), ())),
        precision=lax.Precision.HIGHEST,
        preferred_element_type=jnp.float32,
    ) * jnp.sqrt(1.0 - decay * decay)
    gathered[pl.ds(me, 1)] = drive.reshape(1, 1, state)
    pl.semaphore_wait(barrier, count - 1)

    def copy_to(step):
        return pltpu.make_async_remote_copy(
            src_ref=gathered.at[me],
            dst_ref=gathered.at[me],
            send_sem=send_sem.at[step],
            recv_sem=recv_sem.at[me],
            device_id={"tm": lax.rem(me + step, count)},
            device_id_type=pl.DeviceIdType.MESH,
        )

    def send(step, carry):
        copy_to(step).start()
        return carry

    lax.fori_loop(1, count, send, 0)

    forward = (decay * jnp.cos(angle), decay * jnp.sin(angle))
    backward = (back_decay * jnp.cos(back_angle), back_decay * jnp.sin(back_angle))
    both = complex_times(forward, backward)
    frame = lax.broadcasted_iota(jnp.int32, (count, state), 0)
    one = (jnp.ones((1, state), jnp.float32), jnp.zeros((1, state), jnp.float32))
    power, partial = one, one
    partial_sums = [one]
    for _ in range(count - 1):
        power = complex_times(power, both)
        partial = (partial[0] + power[0], partial[1] + power[1])
        partial_sums.append(partial)
    last = jnp.maximum(frame, me)
    sums = [jnp.zeros((count, state), jnp.float32) for _ in range(2)]
    for n in range(count):
        for k in range(2):
            sums[k] = jnp.where(last == count - 1 - n, partial_sums[n][k], sums[k])
    away = jnp.abs(frame - me)
    factor = tuple(jnp.where(frame > me, backward[k], forward[k]) for k in range(2))
    gain = tuple(sums)
    bit = 1
    while bit < count:
        taken = complex_times(gain, factor)
        chosen = (away // bit) % 2 == 1
        gain = tuple(jnp.where(chosen, taken[k], gain[k]) for k in range(2))
        factor = complex_times(factor, factor)
        bit = bit * 2
    weight = jnp.sqrt(1.0 - back_decay * back_decay)
    imaginary = lax.broadcasted_iota(jnp.int32, (count, state), 1) % 2 == 1
    direct = gain[0] * weight
    crossed = jnp.where(imaginary, gain[1], -gain[1]) * weight

    def arrive(step, carry):
        source = lax.rem(me + step, count)
        pltpu.make_async_remote_copy(
            src_ref=gathered.at[source],
            dst_ref=gathered.at[source],
            send_sem=send_sem.at[step],
            recv_sem=recv_sem.at[source],
            device_id={"tm": source},
            device_id_type=pl.DeviceIdType.MESH,
        ).wait_recv()
        return carry

    lax.fori_loop(1, count, arrive, 0)
    drives = gathered[...].reshape(count, state)
    partner = jnp.where(
        imaginary, pltpu.roll(drives, 1, 1), pltpu.roll(drives, state - 1, 1)
    )
    smoothed = jnp.sum(direct * drives + crossed * partner, axis=0, keepdims=True)
    out_ref[...] = lax.dot_general(
        smoothed,
        readout_ref[...],
        (((1,), (1,)), ((), ())),
        precision=lax.Precision.HIGHEST,
        preferred_element_type=jnp.float32,
    )

    def sent(step, carry):
        copy_to(step).wait_send()
        return carry

    lax.fori_loop(1, count, sent, 0)


def filtered_latent(observed, input_map, modes, readout):
    count = lax.axis_size("tm")
    state = observed.shape[1]
    vmem = pl.BlockSpec(memory_space=pltpu.VMEM)
    return pl.pallas_call(
        functools.partial(filter_kernel, count),
        out_shape=jax.ShapeDtypeStruct((1, readout.shape[0]), jnp.float32),
        in_specs=[vmem] * 4,
        out_specs=vmem,
        scratch_shapes=[
            pltpu.VMEM((count, 1, state), jnp.float32),
            pltpu.SemaphoreType.DMA((count,)),
            pltpu.SemaphoreType.DMA((count,)),
        ],
        compiler_params=pltpu.CompilerParams(collective_id=0, has_side_effects=True),
        name="filters",
    )(observed, input_map, modes, readout)


def encode_tiles(frames, patch_weight, depth_weight, point_weight, observe_weight):
    frame_count, height, width = frames.shape
    grid_rows = height // PATCH
    grid_cols = width // PATCH
    channels = patch_weight.shape[1]
    hidden = embed(frames, patch_weight)
    for layer_index in range(LAYERS):
        widened = with_halo(hidden, (("tile", 2),), 1)
        padded = jnp.pad(widened, ((0, 0), (1, 1), (0, 0), (0, 0)))
        hidden = conv_layer(hidden, padded, depth_weight, point_weight, layer_index)
    pooled = jnp.mean(
        hidden.astype(jnp.float32).reshape(
            frame_count, grid_rows // POOL, POOL, grid_cols // POOL, POOL, channels
        ),
        axis=(2, 4),
    ).astype(jnp.bfloat16)
    features = pooled.transpose(0, 2, 1, 3).reshape(frame_count, -1)
    partial_value = jnp.dot(
        features,
        observe_weight.reshape(-1, observe_weight.shape[-1]),
        preferred_element_type=jnp.float32,
    )
    return lax.psum(partial_value, "tile")


def shards(
    movie_frames,
    patch_weight,
    depth_weight,
    point_weight,
    observe_weight,
    input_map,
    mode_decay,
    mode_angle,
    smooth_decay,
    smooth_angle,
    readout,
):
    tile_count = lax.axis_size("tile")
    encoder = (patch_weight, depth_weight, point_weight, observe_weight)
    if tile_count == 1:
        observed = encode_whole(movie_frames[0], *encoder)
    else:
        observed = encode_tiles(movie_frames, *encoder)
        share = readout.shape[0] // tile_count
        readout = lax.dynamic_slice_in_dim(readout, lax.axis_index("tile") * share, share, 0)
    modes = jnp.stack([mode_decay, mode_angle, smooth_decay, smooth_angle])
    return filtered_latent(observed, input_map, modes, readout)


def solution(mesh):
    placed = (
        P("tm", None, "tile"),
        P(),
        P(),
        P(),
        P("tile", None, None, None),
        P(),
        P(),
        P(),
        P(),
        P(),
        P(),
    )
    return jax.shard_map(
        shards, mesh=mesh, in_specs=placed, out_specs=P("tm", "tile"), check_vma=False
    )
```

time: 231 us -> 55.6 us (0.24)
  local copies, waits for them, and re-layouts: 69.1 us -> 2.58 us
  matrix products: 61.8 us -> 0 us
  Pallas kernels: 0 us -> 52.1 us
  starting transfers between devices: 44.8 us -> 0 us
  waiting for transfers between devices: 31.2 us -> 0 us
  other arithmetic: 22 us -> 0.57 us
    dot_general x6 -> x0, matrix products: 61.8 us -> none  [the longest x3 55.5 us: conv_layer(): jnp.dot(depthwise, point_weight[layer_index], preferred_element_type=jnp....]
    pallas_call x0 -> x2, Pallas kernels: none -> 52.1 us  [the longest x1 40 us: encode_whole(): pl.pallas_call(encoder_kernel, out_shape=jax.ShapeDtypeStruct((1, compone...]
    ppermute x18 -> x0, starting transfers between devices: 44.8 us -> none  [the longest x12 40.7 us: passed_along(): return lax.ppermute(x, axis, pairs)]
    reshape x1, local copies, waits for them, and re-layouts: 42.1 us -> 1.36 us  [encode_whole(): depth_weight.reshape(-1, channels)]
    ppermute x18 -> x0, waiting for transfers between devices: 31.2 us -> none  [the longest x12 31.2 us: passed_along(): return lax.ppermute(x, axis, pairs)]
    transpose x2 -> x0, local copies, waits for them, and re-layouts: 24 us -> none  [the longest x1 24 us: embed(): patches = frames.reshape(frame_count, grid_rows, PATCH, grid_cols, PATCH)...]
    concatenate x3 -> x0, other arithmetic: 18.4 us -> none  [with_halo(): x = jnp.concatenate([before, x, after], axis=dim)]
    reduce_sum x1 -> x0, other arithmetic: 3.07 us -> none  [shards(): jnp.mean(hidden.astype(jnp.float32).reshape(frame_count, grid_rows // POO...]
  transfers between devices with their start and end apart: 18 -> 0, of which waited for: 12 -> 0; matrix products, arithmetic and copies ran while one was open for 0% -> 0% of each run, Pallas kernels for 0% -> 0%
where the time goes in v1:
time: 55.6 us; the launch traced here: 55.3 us
  Pallas kernels  52.1 us (94%)
  local copies, waits for them, and re-layouts  2.58 us (5%)
  other arithmetic  0.57 us (1%)
    pallas_call x1, Pallas kernels, encode_whole(): pl.pallas_call(encoder_kernel, out_shape=jax.ShapeDtypeStruct((1, compone...  40 us
    pallas_call x1, Pallas kernels, filtered_latent(): pl.pallas_call(functools.partial(filter_kernel, count), out_shape=jax.Sha...  12.2 us
    reshape x1, local copies, waits for them, and re-layouts, encode_whole(): depth_weight.reshape(-1, channels)  1.36 us
    unnamed x9, local copies, waits for them, and re-layouts  1.21 us

profile of v1, /device:TPU:0, one launch (start us, length us, event | category | flops | bytes accessed | tf_op | source)
XLA Modules:
  0.0 55.3 jit_solution(17697274856854961051)
XLA Ops:
  0.0 0.0 copy-start.3
  0.0 0.0 copy-start.2
  0.0 0.0 copy-start.1
  0.0 0.0 copy-start
  0.0 1.4 %reshape.6.depth_ref = bf16[27,128]{1,0:T(8,128)(2,1)} reshape(bf16[3,3,3,128]{3,2,1,0:T(4,128)(2,1)} %param.13) | data formatting | bytes 13824 | tf_op jit(solution)/shard_map/reshape | solution.py:277
  1.4 40.0 %encoder.1.observed_ref = f32[1,256]{1,0:T(1,128)} custom-call(bf16[1024,1024]{1,0:T(8,128)(2,1)} %bitcast.7, bf16[64,128]{1,0:T(8,128)(2,1)} %patch_ref.1, bf16[27,128]{1,0:T(8,128)(2,1)} %reshape.6.depth_ref, bf16[3,128,128]{2,1,0:T(8,128)(2,1)} %point_ref.1, bf16[16,2048,256]{2,1,0:T(8,128)(2,1)} %bitcast.6), custom_call_target="tpu_custom_call" | custom-call | tf_op jit(solution)/shard_map/encoder/pallas_call | solution.py:259
  41.4 0.0 copy-done.3
  41.4 0.0 copy-done.2
  41.4 0.0 copy-done.1
  41.4 0.0 copy-done
  41.4 0.6 %pad_maximum_fusion.modes_ref = f32[4,128]{1,0:T(4,128)} fusion(f32[1,128]{1,0:T(1,128)S(1)} %bitcast.8, f32[1,128]{1,0:T(1,128)S(1)} %bitcast.9, f32[1,128]{1,0:T(1,128)S(1)} %bitcast.10, f32[1,128]{1,0:T(1,128)S(1)} %bitcast.11), kind=kLoop, calls=%fused_computation | loop fusion | flops 1536 | bytes 4096 | tf_op jit(solution)/shard_map/stack | solution.py:468
  42.0 12.2 %filters.1 = f32[1,256]{1,0:T(1,128)} custom-call(f32[1,256]{1,0:T(1,128)} %encoder.1.observed_ref, f32[256,256]{1,0:T(8,128)} %map_ref.1, f32[4,128]{1,0:T(4,128)} %pad_maximum_fusion.modes_ref, f32[256,256]{1,0:T(8,128)} %readout_ref.1), custom_call_target="tpu_custom_call" | custom-call | tf_op jit(solution)/shard_map/filters/pallas_call | solution.py:407
  54.1 1.2 %copy.13 = f32[1,256]{1,0:T(1,128)} copy(f32[1,256]{1,0:T(1,128)} %filters.1) | data formatting | bytes 2048
Async XLA Ops:
  0.0 41.4 %copy-start.3 = (f32[128]{0:T(128)S(1)}, f32[128]{0:T(128)}, u32[]{:S(2)}) copy-start(f32[128]{0:T(128)} %param.17) | copy-start | bytes 1540
  0.0 41.4 %copy-start.2 = (f32[128]{0:T(128)S(1)}, f32[128]{0:T(128)}, u32[]{:S(2)}) copy-start(f32[128]{0:T(128)} %param.18) | copy-start | bytes 1540
  0.0 41.4 %copy-start.1 = (f32[128]{0:T(128)S(1)}, f32[128]{0:T(128)}, u32[]{:S(2)}) copy-start(f32[128]{0:T(128)} %param.19) | copy-start | bytes 1540
  0.0 41.4 %copy-start = (f32[128]{0:T(128)S(1)}, f32[128]{0:T(128)}, u32[]{:S(2)}) copy-start(f32[128]{0:T(128)} %param.20) | copy-start | bytes 1540

commit v2 on v1

--- a/solution.py
+++ b/solution.py
@@ -79,6 +79,7 @@
     point_ref,
     observe_ref,
     out_ref,
+    frame,
     cells,
     spread,
     first,
@@ -87,6 +88,7 @@
     depth_rows,
     point_pair,
     observe,
+    frame_sem,
     observe_sem,
 ):
     height, width = frame_ref.shape
@@ -101,6 +103,14 @@
             observe_ref.at[index], observe.at[index], observe_sem.at[index]
         )
 
+    row_block = 256
+
+    def frame_copy(index):
+        taken = pl.ds(index * row_block, row_block)
+        return pltpu.make_async_copy(frame_ref.at[taken], frame.at[taken], frame_sem.at[index])
+
+    for index in range(height // row_block):
+        frame_copy(index).start()
     for index in range(pool_cols):
         observe_copy(index).start()
 
@@ -125,9 +135,13 @@
         point_pair[layer, channels:, channels:] = point
         point_pair[layer, :channels, channels:] = square
         point_pair[layer, channels:, :channels] = square
-    depth = depth_ref[...].astype(jnp.float32)
-    for tap in range(LAYERS * 9):
-        depth_rows[tap] = jnp.broadcast_to(depth[tap : tap + 1], (STRIP, channels))
+    for layer in range(LAYERS):
+        for dr in range(3):
+            taps = depth_ref[layer, dr].astype(jnp.float32)
+            for dc in range(3):
+                depth_rows[(layer * 3 + dr) * 3 + dc] = jnp.broadcast_to(
+                    taps[dc : dc + 1], (8, channels)
+                )
 
     for ref in (first, second):
         column = jnp.zeros(ref.shape[1:], jnp.float32)
@@ -137,7 +151,6 @@
         ref[:, :EDGE, :] = edge
         ref[:, EDGE + rows :, :] = edge
 
-    row_block = 256
     row_cells = row_block // PATCH
     to_row = lax.broadcasted_iota(jnp.int32, (row_block, row_block), 0)
     from_row = lax.broadcasted_iota(jnp.int32, (row_block, row_block), 1)
@@ -147,9 +160,10 @@
         0.0,
     ).astype(jnp.bfloat16)
     for b in range(height // row_block):
+        frame_copy(b).wait()
         ordered = jnp.dot(
             order,
-            frame_ref[b * row_block : (b + 1) * row_block, :],
+            frame[b * row_block : (b + 1) * row_block, :],
             preferred_element_type=jnp.float32,
         ).astype(jnp.bfloat16)
         for g in range(lane_groups):
@@ -169,7 +183,6 @@
         half = jnp.dot(taken, spread[n], preferred_element_type=jnp.float32)
         for g in range(half_groups):
             value = gelu_of_half(half[g * rows : (g + 1) * rows])
-            value = value.astype(jnp.bfloat16).astype(jnp.float32)
             column = (part * half_groups + g) * group_cols + 2 * n + 1
             first[column, EDGE : EDGE + rows, :] = value[:, :channels]
             first[column + 1, EDGE : EDGE + rows, :] = value[:, channels:]
@@ -177,50 +190,48 @@
 
     lax.fori_loop(0, (group_cols // 2) * (lane_groups // half_groups), embed_step, 0)
 
-    def layer_branch(layer, source, group):
+    def mix_cells(layer, source, group):
         start = group * GROUP
-        for p in range(GROUP // 2):
-            for strip in range(rows // STRIP):
-                sums = [None, None]
+        weights = []
+        for tap in range(9):
+            one_tile = depth_rows[layer * 9 + tap]
+            weights.append(jnp.concatenate([one_tile] * (STRIP // 8), axis=0))
+        for strip in range(rows // STRIP):
+            sums = [None] * GROUP
+            for cc in range(GROUP + 2):
                 for dr in range(3):
-                    for cc in range(4):
-                        taken = source[
-                            start + 2 * p + cc, pl.ds(EDGE - 1 + strip * STRIP + dr, STRIP), :
-                        ]
-                        for o in range(2):
-                            dc = cc - o
-                            if 0 <= dc <= 2:
-                                term = taken * depth_rows[layer * 9 + dr * 3 + dc]
-                                sums[o] = term if sums[o] is None else sums[o] + term
-                for o in range(2):
-                    mixed[
-                        p * rows + strip * STRIP : p * rows + (strip + 1) * STRIP,
-                        o * channels : (o + 1) * channels,
-                    ] = sums[o].astype(jnp.bfloat16)
+                    taken = source[start + cc, pl.ds(EDGE - 1 + strip * STRIP + dr, STRIP), :]
+                    for dc in range(3):
+                        o = cc - dc
+                        if 0 <= o < GROUP:
+                            term = taken * weights[dr * 3 + dc]
+                            sums[o] = term if sums[o] is None else sums[o] + term
+                if cc >= 2:
+                    o = cc - 2
+                    at = (o // 2) * rows + strip * STRIP
+                    mixed[at : at + STRIP, (o % 2) * channels : (o % 2 + 1) * channels] = sums[
+                        o
+                    ].astype(jnp.bfloat16)
+
+    def mix_channels(layer):
         return jnp.dot(mixed[...], point_pair[layer], preferred_element_type=jnp.float32)
 
-    def updated(source, group, half, p, o):
-        column = group * GROUP + 2 * p + o + 1
+    def updated(source, group, half, o):
+        p = o // 2
         branch = gelu_of_half(
-            half[p * rows : (p + 1) * rows, o * channels : (o + 1) * channels]
-        )
-        value = source[column, EDGE : EDGE + rows, :] + branch
-        return column, value.astype(jnp.bfloat16).astype(jnp.float32)
-
-    def layer_step(layer, source, target, group, carry):
-        half = layer_branch(layer, source, group)
-        for p in range(GROUP // 2):
-            for o in range(2):
-                column, value = updated(source, group, half, p, o)
-                target[column, EDGE : EDGE + rows, :] = value
+            half[p * rows : (p + 1) * rows, (o % 2) * channels : (o % 2 + 1) * channels]
+        )
+        return source[group * GROUP + o + 1, EDGE : EDGE + rows, :] + branch
+
+    def finish(target, source, group, half, carry):
+        for o in range(GROUP):
+            target[group * GROUP + o + 1, EDGE : EDGE + rows, :] = updated(source, group, half, o)
         return carry
 
-    def last_step(source, group, total):
-        half = layer_branch(LAYERS - 1, source, group)
+    def finish_pooled(source, group, half, total):
         summed = jnp.zeros((rows, channels), jnp.float32)
-        for p in range(GROUP // 2):
-            for o in range(2):
-                summed = summed + updated(source, group, half, p, o)[1]
+        for o in range(GROUP):
+            summed = summed + updated(source, group, half, o)
         pooled = jnp.sum(summed.reshape(pool_rows, POOL, channels), axis=1) * (
             1.0 / (POOL * POOL)
         )
@@ -231,18 +242,27 @@
         observe_copy(group).wait()
         return total + jnp.dot(features, observe[group], preferred_element_type=jnp.float32)
 
+    def run_layer(layer, source, finish, carry):
+        groups = cols // GROUP
+        mix_cells(layer, source, 0)
+
+        def step(group, carry):
+            half = mix_channels(layer)
+            mix_cells(layer, source, group)
+            return finish(source, group - 1, half, carry)
+
+        carry = lax.fori_loop(1, groups, step, carry)
+        return finish(source, groups - 1, mix_channels(layer), carry)
+
     refs = (first, second)
     for layer in range(LAYERS - 1):
-        lax.fori_loop(
-            0,
-            cols // GROUP,
-            functools.partial(layer_step, layer, refs[layer % 2], refs[(layer + 1) % 2]),
-            0,
-        )
-    total = lax.fori_loop(
-        0,
-        pool_cols,
-        functools.partial(last_step, refs[(LAYERS - 1) % 2]),
+        run_layer(
+            layer, refs[layer % 2], functools.partial(finish, refs[(layer + 1) % 2]), 0
+        )
+    total = run_layer(
+        LAYERS - 1,
+        refs[(LAYERS - 1) % 2],
+        finish_pooled,
         jnp.zeros((pool_rows, observe.shape[2]), jnp.float32),
     )
     out_ref[...] = jnp.sum(total, axis=0, keepdims=True)
@@ -255,26 +275,29 @@
     pool_cols, pool_rows, _, components = observe_weight.shape
     observe_weight = observe_weight.reshape(pool_cols, pool_rows * channels, components)
     vmem = pl.BlockSpec(memory_space=pltpu.VMEM)
+    anywhere = pl.BlockSpec(memory_space=pl.ANY)
     padded = (cols + 2, rows + 2 * EDGE, channels)
     return pl.pallas_call(
         encoder_kernel,
         out_shape=jax.ShapeDtypeStruct((1, components), jnp.float32),
-        in_specs=[vmem, vmem, vmem, vmem, pl.BlockSpec(memory_space=pl.ANY)],
+        in_specs=[anywhere, vmem, vmem, vmem, anywhere],
         out_specs=vmem,
         scratch_shapes=[
+            pltpu.VMEM((height, width), jnp.bfloat16),
             pltpu.VMEM((width // 128, rows, PATCH * 128), jnp.bfloat16),
             pltpu.VMEM((128 // PATCH // 2, PATCH * 128, 2 * channels), jnp.bfloat16),
             pltpu.VMEM(padded, jnp.float32),
             pltpu.VMEM(padded, jnp.float32),
             pltpu.VMEM((GROUP // 2 * rows, 2 * channels), jnp.bfloat16),
-            pltpu.VMEM((LAYERS * 9, STRIP, channels), jnp.float32),
+            pltpu.VMEM((LAYERS * 9, 8, channels), jnp.float32),
             pltpu.VMEM((LAYERS, 2 * channels, 2 * channels), jnp.bfloat16),
             pltpu.VMEM(observe_weight.shape, jnp.bfloat16),
+            pltpu.SemaphoreType.DMA((height // 256,)),
             pltpu.SemaphoreType.DMA((pool_cols,)),
         ],
         compiler_params=pltpu.CompilerParams(vmem_limit_bytes=60 * 1024 * 1024),
         name="encoder",
-    )(frame, patch_weight, depth_weight.reshape(-1, channels), point_weight, observe_weight)
+    )(frame, patch_weight, depth_weight, point_weight, observe_weight)
 
 
 def complex_times(a, b):
@@ -282,7 +305,17 @@
 
 
 def filter_kernel(
-    count, observed_ref, map_ref, modes_ref, readout_ref, out_ref, gathered, send_sem, recv_sem
+    count,
+    observed_ref,
+    map_ref,
+    decay_ref,
+    angle_ref,
+    back_decay_ref,
+    back_angle_ref,
+    out_ref,
+    gathered,
+    send_sem,
+    recv_sem,
 ):
     me = lax.axis_index("tm")
     barrier = pltpu.get_barrier_semaphore()
@@ -298,13 +331,14 @@
 
     lax.fori_loop(1, count, greet, 0)
 
-    modes = modes_ref.shape[1]
+    mode_refs = (decay_ref, angle_ref, back_decay_ref, back_angle_ref)
+    modes = decay_ref.shape[1]
     state = 2 * modes
     mode = lax.broadcasted_iota(jnp.int32, (modes, state), 0)
     component = lax.broadcasted_iota(jnp.int32, (modes, state), 1)
     repeat = jnp.where(component // 2 == mode, 1.0, 0.0)
     doubled = jnp.dot(
-        modes_ref[...],
+        jnp.concatenate([ref[...] for ref in mode_refs], axis=0),
         repeat,
         precision=lax.Precision.HIGHEST,
         preferred_element_type=jnp.float32,
@@ -384,14 +418,7 @@
     partner = jnp.where(
         imaginary, pltpu.roll(drives, 1, 1), pltpu.roll(drives, state - 1, 1)
     )
-    smoothed = jnp.sum(direct * drives + crossed * partner, axis=0, keepdims=True)
-    out_ref[...] = lax.dot_general(
-        smoothed,
-        readout_ref[...],
-        (((1,), (1,)), ((), ())),
-        precision=lax.Precision.HIGHEST,
-        preferred_element_type=jnp.float32,
-    )
+    out_ref[...] = jnp.sum(direct * drives + crossed * partner, axis=0, keepdims=True)
 
     def sent(step, carry):
         copy_to(step).wait_send()
@@ -400,14 +427,14 @@
     lax.fori_loop(1, count, sent, 0)
 
 
-def filtered_latent(observed, input_map, modes, readout):
+def smoothed_state(observed, input_map, *modes):
     count = lax.axis_size("tm")
-    state = observed.shape[1]
+    state = input_map.shape[0]
     vmem = pl.BlockSpec(memory_space=pltpu.VMEM)
     return pl.pallas_call(
         functools.partial(filter_kernel, count),
-        out_shape=jax.ShapeDtypeStruct((1, readout.shape[0]), jnp.float32),
-        in_specs=[vmem] * 4,
+        out_shape=jax.ShapeDtypeStruct((1, state), jnp.float32),
+        in_specs=[vmem] * 6,
         out_specs=vmem,
         scratch_shapes=[
             pltpu.VMEM((count, 1, state), jnp.float32),
@@ -416,7 +443,7 @@
         ],
         compiler_params=pltpu.CompilerParams(collective_id=0, has_side_effects=True),
         name="filters",
-    )(observed, input_map, modes, readout)
+    )(observed, input_map, *(mode.reshape(1, -1) for mode in modes))
 
 
 def encode_tiles(frames, patch_weight, depth_weight, point_weight, observe_weight):
@@ -465,8 +492,10 @@
         observed = encode_tiles(movie_frames, *encoder)
         share = readout.shape[0] // tile_count
         readout = lax.dynamic_slice_in_dim(readout, lax.axis_index("tile") * share, share, 0)
-    modes = jnp.stack([mode_decay, mode_angle, smooth_decay, smooth_angle])
-    return filtered_latent(observed, input_map, modes, readout)
+    smoothed = smoothed_state(
+        observed, input_map, mode_decay, mode_angle, smooth_decay, smooth_angle
+    )
+    return jnp.dot(smoothed, readout.T, precision=lax.Precision.HIGHEST)
 
 
 def solution(mesh):

time: 55.6 us -> 59.7 us (1.074)
  Pallas kernels: 52.1 us -> 57.9 us
  local copies, waits for them, and re-layouts: 2.58 us -> 0.01 us
  matrix products: 0 us -> 1.55 us
    pallas_call x1, Pallas kernels: 40 us -> 46.2 us  [encode_whole(): pl.pallas_call(encoder_kernel, out_shape=jax.ShapeDtypeStruct((1, compone...]
    dot_general x0 -> x1, matrix products: none -> 1.55 us  [shards(): return jnp.dot(smoothed, readout.T, precision=lax.Precision.HIGHEST)]
    reshape x1 -> x0, local copies, waits for them, and re-layouts: 1.36 us -> none  [encode_whole(): depth_weight.reshape(-1, channels)]
    unnamed x9 -> x2, local copies, waits for them, and re-layouts: 1.21 us -> 0.01 us
where the time goes in v2:
time: 59.7 us; the launch traced here: 59.5 us
  Pallas kernels  57.9 us (97%)
  matrix products  1.55 us (3%)
    pallas_call x1, Pallas kernels, encode_whole(): pl.pallas_call(encoder_kernel, out_shape=jax.ShapeDtypeStruct((1, compone...  46.2 us
    pallas_call x1, Pallas kernels, smoothed_state(): pl.pallas_call(functools.partial(filter_kernel, count), out_shape=jax.Sha...  11.7 us
    dot_general x1, matrix products, shards(): return jnp.dot(smoothed, readout.T, precision=lax.Precision.HIGHEST)  1.55 us

profile of v2, /device:TPU:0, one launch (start us, length us, event | category | flops | bytes accessed | tf_op | source)
XLA Modules:
  0.0 59.5 jit_solution(2112447560574199374)
XLA Ops:
  0.0 0.0 copy-start
  0.0 46.2 %encoder.1.observed_ref = f32[1,256]{1,0:T(1,128)} custom-call(bf16[1024,1024]{1,0:T(8,128)(2,1)} %bitcast.13, bf16[64,128]{1,0:T(8,128)(2,1)} %patch_ref.1, bf16[3,3,3,128]{3,2,1,0:T(4,128)(2,1)} %depth_ref.1, bf16[3,128,128]{2,1,0:T(8,128)(2,1)} %point_ref.1, bf16[16,2048,256]{2,1,0:T(8,128)(2,1)} %bitcast.12), custom_call_target="tpu_custom_call" | custom-call | tf_op jit(solution)/shard_map/encoder/pallas_call | solution.py:280
  46.2 11.7 %filters.1 = f32[1,256]{1,0:T(1,128)} custom-call(f32[1,256]{1,0:T(1,128)} %encoder.1.observed_ref, f32[256,256]{1,0:T(8,128)} %map_ref.1, f32[1,128]{1,0:T(1,128)} %bitcast.14, f32[1,128]{1,0:T(1,128)} %bitcast.15, f32[1,128]{1,0:T(1,128)} %bitcast.16, f32[1,128]{1,0:T(1,128)} %bitcast.17), custom_call_target="tpu_custom_call" | custom-call | tf_op jit(solution)/shard_map/filters/pallas_call | solution.py:434
  57.9 0.0 copy-done
  58.0 1.5 %fusion = f32[1,256]{1,0:T(1,128)} fusion(f32[256,256]{1,0:T(8,128)S(1)} %copy-done, f32[1,256]{1,0:T(1,128)} %filters.1), kind=kOutput, calls=%fused_computation | convolution fusion | flops 786432 | bytes 264192 | tf_op jit(solution)/shard_map/dot_general | solution.py:498
Async XLA Ops:
  0.0 58.0 %copy-start = (f32[256,256]{1,0:T(8,128)S(1)}, f32[256,256]{1,0:T(8,128)}, u32[]{:S(2)}) copy-start(f32[256,256]{1,0:T(8,128)} %param.21) | copy-start | bytes 786436

commit v3 on v2

--- a/solution.py
+++ b/solution.py
@@ -62,9 +62,7 @@
 
 GELU_LINEAR = 2.0 * math.sqrt(2.0 / math.pi)
 GELU_CUBIC = 4.0 * 0.044715 * GELU_LINEAR
-EDGE = 8
 GROUP = 8
-STRIP = 16
 
 
 def gelu_of_half(half):
@@ -97,22 +95,21 @@
     lane_groups = width // 128
     group_cols = 128 // PATCH
     pool_cols, pool_rows = cols // POOL, rows // POOL
+    halves = 2
+    half_height = height // halves
+    half_rows = pool_rows // halves
+
+    def frame_copy(index):
+        taken = pl.ds(index * half_height, half_height)
+        return pltpu.make_async_copy(frame_ref.at[taken], frame.at[taken], frame_sem.at[index])
 
     def observe_copy(index):
         return pltpu.make_async_copy(
             observe_ref.at[index], observe.at[index], observe_sem.at[index]
         )
 
-    row_block = 256
-
-    def frame_copy(index):
-        taken = pl.ds(index * row_block, row_block)
-        return pltpu.make_async_copy(frame_ref.at[taken], frame.at[taken], frame_sem.at[index])
-
-    for index in range(height // row_block):
+    for index in range(halves):
         frame_copy(index).start()
-    for index in range(pool_cols):
-        observe_copy(index).start()
 
     patch = patch_ref[...].astype(jnp.float32) * 0.5
     blank = jnp.zeros((PATCH, channels), jnp.float32)
@@ -140,37 +137,57 @@
             taps = depth_ref[layer, dr].astype(jnp.float32)
             for dc in range(3):
                 depth_rows[(layer * 3 + dr) * 3 + dc] = jnp.broadcast_to(
-                    taps[dc : dc + 1], (8, channels)
-                )
+                    taps[dc : dc + 1], (pool_rows, channels)
+                ).astype(jnp.bfloat16)
 
     for ref in (first, second):
-        column = jnp.zeros(ref.shape[1:], jnp.float32)
+        column = jnp.zeros(ref.shape[1:], jnp.bfloat16)
         ref[0] = column
         ref[cols + 1] = column
-        edge = jnp.zeros((cols + 2, EDGE, channels), jnp.float32)
-        ref[:, :EDGE, :] = edge
-        ref[:, EDGE + rows :, :] = edge
-
-    row_cells = row_block // PATCH
-    to_row = lax.broadcasted_iota(jnp.int32, (row_block, row_block), 0)
-    from_row = lax.broadcasted_iota(jnp.int32, (row_block, row_block), 1)
-    order = jnp.where(
-        (from_row % PATCH == to_row // row_cells) & (from_row // PATCH == to_row % row_cells),
-        1.0,
-        0.0,
-    ).astype(jnp.bfloat16)
-    for b in range(height // row_block):
-        frame_copy(b).wait()
-        ordered = jnp.dot(
-            order,
-            frame[b * row_block : (b + 1) * row_block, :],
-            preferred_element_type=jnp.float32,
-        ).astype(jnp.bfloat16)
-        for g in range(lane_groups):
-            for i in range(PATCH):
-                cells[
-                    g, b * row_cells : (b + 1) * row_cells, i * 128 : (i + 1) * 128
-                ] = ordered[i * row_cells : (i + 1) * row_cells, g * 128 : (g + 1) * 128]
+
+    to_row = lax.broadcasted_iota(jnp.int32, (half_height, half_height), 0)
+    from_row = lax.broadcasted_iota(jnp.int32, (half_height, half_height), 1)
+    place = to_row // half_rows
+    source_row = (to_row % half_rows) * (POOL * PATCH) + (place % POOL) * PATCH + place // POOL
+    order = jnp.where(from_row == source_row, 1.0, 0.0).astype(jnp.bfloat16)
+    for index in range(halves):
+        frame_copy(index).wait()
+    for index in range(pool_cols):
+        observe_copy(index).start()
+    for pair in range(lane_groups // 2):
+        lanes = slice(pair * 256, (pair + 1) * 256)
+        ordered = [
+            jnp.dot(
+                order,
+                frame[h * half_height : (h + 1) * half_height, lanes],
+                preferred_element_type=jnp.float32,
+            )
+            for h in range(halves)
+        ]
+        for i in range(PATCH):
+            for q in range(POOL):
+                at = (i * POOL + q) * half_rows
+                tile = jnp.concatenate(
+                    [part[at : at + half_rows] for part in ordered], axis=0
+                ).astype(jnp.bfloat16)
+                for g in range(2):
+                    cells[
+                        pair * 2 + g,
+                        q * pool_rows : (q + 1) * pool_rows,
+                        i * 128 : (i + 1) * 128,
+                    ] = tile[:, g * 128 : (g + 1) * 128]
+
+    sublane = lax.broadcasted_iota(jnp.int32, (pool_rows, channels), 0)
+
+    def store_column(target, column, tiles):
+        for q in range(POOL):
+            target[column, q + 1] = tiles[q].astype(jnp.bfloat16)
+        above = pltpu.roll(tiles[POOL - 1], 1, 0)
+        below = pltpu.roll(tiles[0], pool_rows - 1, 0)
+        target[column, 0] = jnp.where(sublane == 0, 0.0, above).astype(jnp.bfloat16)
+        target[column, POOL + 1] = jnp.where(sublane == pool_rows - 1, 0.0, below).astype(
+            jnp.bfloat16
+        )
 
     half_groups = max(lane_groups // 2, 1)
 
@@ -182,62 +199,69 @@
         )
         half = jnp.dot(taken, spread[n], preferred_element_type=jnp.float32)
         for g in range(half_groups):
-            value = gelu_of_half(half[g * rows : (g + 1) * rows])
             column = (part * half_groups + g) * group_cols + 2 * n + 1
-            first[column, EDGE : EDGE + rows, :] = value[:, :channels]
-            first[column + 1, EDGE : EDGE + rows, :] = value[:, channels:]
+            for o in range(2):
+                tiles = [
+                    gelu_of_half(
+                        half[
+                            g * rows + q * pool_rows : g * rows + (q + 1) * pool_rows,
+                            o * channels : (o + 1) * channels,
+                        ]
+                    )
+                    for q in range(POOL)
+                ]
+                store_column(first, column + o, tiles)
         return carry
 
     lax.fori_loop(0, (group_cols // 2) * (lane_groups // half_groups), embed_step, 0)
 
     def mix_cells(layer, source, group):
         start = group * GROUP
-        weights = []
-        for tap in range(9):
-            one_tile = depth_rows[layer * 9 + tap]
-            weights.append(jnp.concatenate([one_tile] * (STRIP // 8), axis=0))
-        for strip in range(rows // STRIP):
+        weights = [depth_rows[layer * 9 + tap] for tap in range(9)]
+        for q in range(POOL):
             sums = [None] * GROUP
             for cc in range(GROUP + 2):
-                for dr in range(3):
-                    taken = source[start + cc, pl.ds(EDGE - 1 + strip * STRIP + dr, STRIP), :]
-                    for dc in range(3):
-                        o = cc - dc
-                        if 0 <= o < GROUP:
-                            term = taken * weights[dr * 3 + dc]
-                            sums[o] = term if sums[o] is None else sums[o] + term
+                taken = [source[start + cc, q + dr] for dr in range(3)]
+                for dc in range(3):
+                    o = cc - dc
+                    if 0 <= o < GROUP:
+                        term = (
+                            taken[0] * weights[dc] + taken[1] * weights[3 + dc]
+                        ) + taken[2] * weights[6 + dc]
+                        sums[o] = term if sums[o] is None else sums[o] + term
                 if cc >= 2:
                     o = cc - 2
-                    at = (o // 2) * rows + strip * STRIP
-                    mixed[at : at + STRIP, (o % 2) * channels : (o % 2 + 1) * channels] = sums[
-                        o
-                    ].astype(jnp.bfloat16)
+                    at = (o // 2) * rows + q * pool_rows
+                    mixed[
+                        at : at + pool_rows, (o % 2) * channels : (o % 2 + 1) * channels
+                    ] = sums[o]
 
     def mix_channels(layer):
         return jnp.dot(mixed[...], point_pair[layer], preferred_element_type=jnp.float32)
 
     def updated(source, group, half, o):
-        p = o // 2
-        branch = gelu_of_half(
-            half[p * rows : (p + 1) * rows, (o % 2) * channels : (o % 2 + 1) * channels]
-        )
-        return source[group * GROUP + o + 1, EDGE : EDGE + rows, :] + branch
+        tiles = []
+        for q in range(POOL):
+            at = (o // 2) * rows + q * pool_rows
+            branch = gelu_of_half(
+                half[at : at + pool_rows, (o % 2) * channels : (o % 2 + 1) * channels]
+            )
+            tiles.append(source[group * GROUP + o + 1, q + 1].astype(jnp.float32) + branch)
+        return tiles
 
     def finish(target, source, group, half, carry):
         for o in range(GROUP):
-            target[group * GROUP + o + 1, EDGE : EDGE + rows, :] = updated(source, group, half, o)
+            store_column(target, group * GROUP + o + 1, updated(source, group, half, o))
         return carry
 
     def finish_pooled(source, group, half, total):
-        summed = jnp.zeros((rows, channels), jnp.float32)
+        summed = jnp.zeros((pool_rows, channels), jnp.float32)
         for o in range(GROUP):
-            summed = summed + updated(source, group, half, o)
-        pooled = jnp.sum(summed.reshape(pool_rows, POOL, channels), axis=1) * (
-            1.0 / (POOL * POOL)
-        )
-        own = lax.broadcasted_iota(jnp.int32, (pool_rows, channels), 0)
+            for tile in updated(source, group, half, o):
+                summed = summed + tile
+        pooled = summed * (1.0 / (POOL * POOL))
         features = jnp.concatenate(
-            [jnp.where(own == r, pooled, 0.0) for r in range(pool_rows)], axis=1
+            [jnp.where(sublane == r, pooled, 0.0) for r in range(pool_rows)], axis=1
         ).astype(jnp.bfloat16)
         observe_copy(group).wait()
         return total + jnp.dot(features, observe[group], preferred_element_type=jnp.float32)
@@ -276,7 +300,7 @@
     observe_weight = observe_weight.reshape(pool_cols, pool_rows * channels, components)
     vmem = pl.BlockSpec(memory_space=pltpu.VMEM)
     anywhere = pl.BlockSpec(memory_space=pl.ANY)
-    padded = (cols + 2, rows + 2 * EDGE, channels)
+    padded = (cols + 2, POOL + 2, pool_rows, channels)
     return pl.pallas_call(
         encoder_kernel,
         out_shape=jax.ShapeDtypeStruct((1, components), jnp.float32),
@@ -286,13 +310,13 @@
             pltpu.VMEM((height, width), jnp.bfloat16),
             pltpu.VMEM((width // 128, rows, PATCH * 128), jnp.bfloat16),
             pltpu.VMEM((128 // PATCH // 2, PATCH * 128, 2 * channels), jnp.bfloat16),
-            pltpu.VMEM(padded, jnp.float32),
-            pltpu.VMEM(padded, jnp.float32),
+            pltpu.VMEM(padded, jnp.bfloat16),
+            pltpu.VMEM(padded, jnp.bfloat16),
             pltpu.VMEM((GROUP // 2 * rows, 2 * channels), jnp.bfloat16),
-            pltpu.VMEM((LAYERS * 9, 8, channels), jnp.float32),
+            pltpu.VMEM((LAYERS * 9, pool_rows, channels), jnp.bfloat16),
             pltpu.VMEM((LAYERS, 2 * channels, 2 * channels), jnp.bfloat16),
             pltpu.VMEM(observe_weight.shape, jnp.bfloat16),
-            pltpu.SemaphoreType.DMA((height // 256,)),
+            pltpu.SemaphoreType.DMA((2,)),
             pltpu.SemaphoreType.DMA((pool_cols,)),
         ],
         compiler_params=pltpu.CompilerParams(vmem_limit_bytes=60 * 1024 * 1024),

time: 59.7 us -> 56.2 us (0.941)
  Pallas kernels: 57.9 us -> 54.5 us
    pallas_call x1, Pallas kernels: 46.2 us -> 42.7 us  [encode_whole(): pl.pallas_call(encoder_kernel, out_shape=jax.ShapeDtypeStruct((1, compone...]
where the time goes in v3:
time: 56.2 us; the launch traced here: 56.1 us
  Pallas kernels  54.5 us (97%)
  matrix products  1.55 us (3%)
    pallas_call x1, Pallas kernels, encode_whole(): pl.pallas_call(encoder_kernel, out_shape=jax.ShapeDtypeStruct((1, compone...  42.7 us
    pallas_call x1, Pallas kernels, smoothed_state(): pl.pallas_call(functools.partial(filter_kernel, count), out_shape=jax.Sha...  11.7 us
    dot_general x1, matrix products, shards(): return jnp.dot(smoothed, readout.T, precision=lax.Precision.HIGHEST)  1.55 us

profile of v3, /device:TPU:0, one launch (start us, length us, event | category | flops | bytes accessed | tf_op | source)
XLA Modules:
  0.0 56.1 jit_solution(9690051383996232314)
XLA Ops:
  0.0 0.0 copy-start
  0.0 42.7 %encoder.1.observed_ref = f32[1,256]{1,0:T(1,128)} custom-call(bf16[1024,1024]{1,0:T(8,128)(2,1)} %bitcast.13, bf16[64,128]{1,0:T(8,128)(2,1)} %patch_ref.1, bf16[3,3,3,128]{3,2,1,0:T(4,128)(2,1)} %depth_ref.1, bf16[3,128,128]{2,1,0:T(8,128)(2,1)} %point_ref.1, bf16[16,2048,256]{2,1,0:T(8,128)(2,1)} %bitcast.12), custom_call_target="tpu_custom_call" | custom-call | tf_op jit(solution)/shard_map/encoder/pallas_call | solution.py:304
  42.7 11.7 %filters.1 = f32[1,256]{1,0:T(1,128)} custom-call(f32[1,256]{1,0:T(1,128)} %encoder.1.observed_ref, f32[256,256]{1,0:T(8,128)} %map_ref.1, f32[1,128]{1,0:T(1,128)} %bitcast.14, f32[1,128]{1,0:T(1,128)} %bitcast.15, f32[1,128]{1,0:T(1,128)} %bitcast.16, f32[1,128]{1,0:T(1,128)} %bitcast.17), custom_call_target="tpu_custom_call" | custom-call | tf_op jit(solution)/shard_map/filters/pallas_call | solution.py:458
  54.5 0.0 copy-done
  54.5 1.5 %fusion = f32[1,256]{1,0:T(1,128)} fusion(f32[256,256]{1,0:T(8,128)S(1)} %copy-done, f32[1,256]{1,0:T(1,128)} %filters.1), kind=kOutput, calls=%fused_computation | convolution fusion | flops 786432 | bytes 264192 | tf_op jit(solution)/shard_map/dot_general | solution.py:522
Async XLA Ops:
  0.0 54.5 %copy-start = (f32[256,256]{1,0:T(8,128)S(1)}, f32[256,256]{1,0:T(8,128)}, u32[]{:S(2)}) copy-start(f32[256,256]{1,0:T(8,128)} %param.21) | copy-start | bytes 786436

commit v4 on v3

--- a/solution.py
+++ b/solution.py
@@ -63,6 +63,10 @@
 GELU_LINEAR = 2.0 * math.sqrt(2.0 / math.pi)
 GELU_CUBIC = 4.0 * 0.044715 * GELU_LINEAR
 GROUP = 8
+
+
+def log2(size):
+    return size.bit_length() - 1
 
 
 def gelu_of_half(half):
@@ -147,8 +151,12 @@
 
     to_row = lax.broadcasted_iota(jnp.int32, (half_height, half_height), 0)
     from_row = lax.broadcasted_iota(jnp.int32, (half_height, half_height), 1)
-    place = to_row // half_rows
-    source_row = (to_row % half_rows) * (POOL * PATCH) + (place % POOL) * PATCH + place // POOL
+    place = to_row >> log2(half_rows)
+    source_row = (
+        ((to_row & (half_rows - 1)) << log2(POOL * PATCH))
+        + ((place & (POOL - 1)) << log2(PATCH))
+        + (place >> log2(POOL))
+    )
     order = jnp.where(from_row == source_row, 1.0, 0.0).astype(jnp.bfloat16)
     for index in range(halves):
         frame_copy(index).wait()
@@ -360,7 +368,7 @@
     state = 2 * modes
     mode = lax.broadcasted_iota(jnp.int32, (modes, state), 0)
     component = lax.broadcasted_iota(jnp.int32, (modes, state), 1)
-    repeat = jnp.where(component // 2 == mode, 1.0, 0.0)
+    repeat = jnp.where(component >> 1 == mode, 1.0, 0.0)
     doubled = jnp.dot(
         jnp.concatenate([ref[...] for ref in mode_refs], axis=0),
         repeat,
@@ -416,12 +424,12 @@
     bit = 1
     while bit < count:
         taken = complex_times(gain, factor)
-        chosen = (away // bit) % 2 == 1
+        chosen = (away & bit) != 0
         gain = tuple(jnp.where(chosen, taken[k], gain[k]) for k in range(2))
         factor = complex_times(factor, factor)
         bit = bit * 2
     weight = jnp.sqrt(1.0 - back_decay * back_decay)
-    imaginary = lax.broadcasted_iota(jnp.int32, (count, state), 1) % 2 == 1
+    imaginary = (lax.broadcasted_iota(jnp.int32, (count, state), 1) & 1) == 1
     direct = gain[0] * weight
     crossed = jnp.where(imaginary, gain[1], -gain[1]) * weight
 

time: 56.2 us -> 56.2 us (level)
  no operation moved by 1% of the time
where the time goes in v4:
time: 56.2 us; the launch traced here: 56 us
  Pallas kernels  54.5 us (97%)
  matrix products  1.55 us (3%)
    pallas_call x1, Pallas kernels, encode_whole(): pl.pallas_call(encoder_kernel, out_shape=jax.ShapeDtypeStruct((1, compone...  42.7 us
    pallas_call x1, Pallas kernels, smoothed_state(): pl.pallas_call(functools.partial(filter_kernel, count), out_shape=jax.Sha...  11.7 us
    dot_general x1, matrix products, shards(): return jnp.dot(smoothed, readout.T, precision=lax.Precision.HIGHEST)  1.55 us

profile of v4, /device:TPU:0, one launch (start us, length us, event | category | flops | bytes accessed | tf_op | source)
XLA Modules:
  0.0 56.0 jit_solution(14793669197564520721)
XLA Ops:
  0.0 0.0 copy-start
  0.0 42.7 %encoder.1.observed_ref = f32[1,256]{1,0:T(1,128)} custom-call(bf16[1024,1024]{1,0:T(8,128)(2,1)} %bitcast.13, bf16[64,128]{1,0:T(8,128)(2,1)} %patch_ref.1, bf16[3,3,3,128]{3,2,1,0:T(4,128)(2,1)} %depth_ref.1, bf16[3,128,128]{2,1,0:T(8,128)(2,1)} %point_ref.1, bf16[16,2048,256]{2,1,0:T(8,128)(2,1)} %bitcast.12), custom_call_target="tpu_custom_call" | custom-call | tf_op jit(solution)/shard_map/encoder/pallas_call | solution.py:312
  42.7 11.7 %filters.1 = f32[1,256]{1,0:T(1,128)} custom-call(f32[1,256]{1,0:T(1,128)} %encoder.1.observed_ref, f32[256,256]{1,0:T(8,128)} %map_ref.1, f32[1,128]{1,0:T(1,128)} %bitcast.14, f32[1,128]{1,0:T(1,128)} %bitcast.15, f32[1,128]{1,0:T(1,128)} %bitcast.16, f32[1,128]{1,0:T(1,128)} %bitcast.17), custom_call_target="tpu_custom_call" | custom-call | tf_op jit(solution)/shard_map/filters/pallas_call | solution.py:466
  54.5 0.0 copy-done
  54.5 1.5 %fusion = f32[1,256]{1,0:T(1,128)} fusion(f32[256,256]{1,0:T(8,128)S(1)} %copy-done, f32[1,256]{1,0:T(1,128)} %filters.1), kind=kOutput, calls=%fused_computation | convolution fusion | flops 786432 | bytes 264192 | tf_op jit(solution)/shard_map/dot_general | solution.py:530
Async XLA Ops:
  0.0 54.5 %copy-start = (f32[256,256]{1,0:T(8,128)S(1)}, f32[256,256]{1,0:T(8,128)}, u32[]{:S(2)}) copy-start(f32[256,256]{1,0:T(8,128)} %param.21) | copy-start | bytes 786436

commit v5 on v4

--- a/solution.py
+++ b/solution.py
@@ -275,16 +275,11 @@
         return total + jnp.dot(features, observe[group], preferred_element_type=jnp.float32)
 
     def run_layer(layer, source, finish, carry):
-        groups = cols // GROUP
-        mix_cells(layer, source, 0)
-
         def step(group, carry):
-            half = mix_channels(layer)
             mix_cells(layer, source, group)
-            return finish(source, group - 1, half, carry)
-
-        carry = lax.fori_loop(1, groups, step, carry)
-        return finish(source, groups - 1, mix_channels(layer), carry)
+            return finish(source, group, mix_channels(layer), carry)
+
+        return lax.fori_loop(0, cols // GROUP, step, carry)
 
     refs = (first, second)
     for layer in range(LAYERS - 1):

time: 56.2 us -> 58 us (1.032)
  Pallas kernels: 54.5 us -> 56.2 us
    pallas_call x1, Pallas kernels: 42.7 us -> 44.4 us  [encode_whole(): pl.pallas_call(encoder_kernel, out_shape=jax.ShapeDtypeStruct((1, compone...]
where the time goes in v5:
time: 58 us; the launch traced here: 57.8 us
  Pallas kernels  56.2 us (97%)
  matrix products  1.55 us (3%)
    pallas_call x1, Pallas kernels, encode_whole(): pl.pallas_call(encoder_kernel, out_shape=jax.ShapeDtypeStruct((1, compone...  44.4 us
    pallas_call x1, Pallas kernels, smoothed_state(): pl.pallas_call(functools.partial(filter_kernel, count), out_shape=jax.Sha...  11.7 us
    dot_general x1, matrix products, shards(): return jnp.dot(smoothed, readout.T, precision=lax.Precision.HIGHEST)  1.55 us

profile of v5, /device:TPU:0, one launch (start us, length us, event | category | flops | bytes accessed | tf_op | source)
XLA Modules:
  0.0 57.8 jit_solution(9473615362136730623)
XLA Ops:
  0.0 0.0 copy-start
  0.0 44.4 %encoder.1.observed_ref = f32[1,256]{1,0:T(1,128)} custom-call(bf16[1024,1024]{1,0:T(8,128)(2,1)} %bitcast.13, bf16[64,128]{1,0:T(8,128)(2,1)} %patch_ref.1, bf16[3,3,3,128]{3,2,1,0:T(4,128)(2,1)} %depth_ref.1, bf16[3,128,128]{2,1,0:T(8,128)(2,1)} %point_ref.1, bf16[16,2048,256]{2,1,0:T(8,128)(2,1)} %bitcast.12), custom_call_target="tpu_custom_call" | custom-call | tf_op jit(solution)/shard_map/encoder/pallas_call | solution.py:307
  44.5 11.7 %filters.1 = f32[1,256]{1,0:T(1,128)} custom-call(f32[1,256]{1,0:T(1,128)} %encoder.1.observed_ref, f32[256,256]{1,0:T(8,128)} %map_ref.1, f32[1,128]{1,0:T(1,128)} %bitcast.14, f32[1,128]{1,0:T(1,128)} %bitcast.15, f32[1,128]{1,0:T(1,128)} %bitcast.16, f32[1,128]{1,0:T(1,128)} %bitcast.17), custom_call_target="tpu_custom_call" | custom-call | tf_op jit(solution)/shard_map/filters/pallas_call | solution.py:461
  56.2 0.0 copy-done
  56.2 1.5 %fusion = f32[1,256]{1,0:T(1,128)} fusion(f32[256,256]{1,0:T(8,128)S(1)} %copy-done, f32[1,256]{1,0:T(1,128)} %filters.1), kind=kOutput, calls=%fused_computation | convolution fusion | flops 786432 | bytes 264192 | tf_op jit(solution)/shard_map/dot_general | solution.py:525
Async XLA Ops:
  0.0 56.2 %copy-start = (f32[256,256]{1,0:T(8,128)S(1)}, f32[256,256]{1,0:T(8,128)}, u32[]{:S(2)}) copy-start(f32[256,256]{1,0:T(8,128)} %param.21) | copy-start | bytes 786436

commit v6 on v1

--- a/solution.py
+++ b/solution.py
@@ -125,9 +125,13 @@
         point_pair[layer, channels:, channels:] = point
         point_pair[layer, :channels, channels:] = square
         point_pair[layer, channels:, :channels] = square
-    depth = depth_ref[...].astype(jnp.float32)
-    for tap in range(LAYERS * 9):
-        depth_rows[tap] = jnp.broadcast_to(depth[tap : tap + 1], (STRIP, channels))
+    for layer in range(LAYERS):
+        for dr in range(3):
+            taps = depth_ref[layer, dr].astype(jnp.float32)
+            for dc in range(3):
+                depth_rows[(layer * 3 + dr) * 3 + dc] = jnp.broadcast_to(
+                    taps[dc : dc + 1], (STRIP, channels)
+                )
 
     for ref in (first, second):
         column = jnp.zeros(ref.shape[1:], jnp.float32)
@@ -274,7 +278,7 @@
         ],
         compiler_params=pltpu.CompilerParams(vmem_limit_bytes=60 * 1024 * 1024),
         name="encoder",
-    )(frame, patch_weight, depth_weight.reshape(-1, channels), point_weight, observe_weight)
+    )(frame, patch_weight, depth_weight, point_weight, observe_weight)
 
 
 def complex_times(a, b):
@@ -282,7 +286,17 @@
 
 
 def filter_kernel(
-    count, observed_ref, map_ref, modes_ref, readout_ref, out_ref, gathered, send_sem, recv_sem
+    count,
+    observed_ref,
+    map_ref,
+    decay_ref,
+    angle_ref,
+    back_decay_ref,
+    back_angle_ref,
+    out_ref,
+    gathered,
+    send_sem,
+    recv_sem,
 ):
     me = lax.axis_index("tm")
     barrier = pltpu.get_barrier_semaphore()
@@ -298,13 +312,14 @@
 
     lax.fori_loop(1, count, greet, 0)
 
-    modes = modes_ref.shape[1]
+    mode_refs = (decay_ref, angle_ref, back_decay_ref, back_angle_ref)
+    modes = decay_ref.shape[1]
     state = 2 * modes
     mode = lax.broadcasted_iota(jnp.int32, (modes, state), 0)
     component = lax.broadcasted_iota(jnp.int32, (modes, state), 1)
-    repeat = jnp.where(component // 2 == mode, 1.0, 0.0)
+    repeat = jnp.where(component >> 1 == mode, 1.0, 0.0)
     doubled = jnp.dot(
-        modes_ref[...],
+        jnp.concatenate([ref[...] for ref in mode_refs], axis=0),
         repeat,
         precision=lax.Precision.HIGHEST,
         preferred_element_type=jnp.float32,
@@ -358,12 +373,12 @@
     bit = 1
     while bit < count:
         taken = complex_times(gain, factor)
-        chosen = (away // bit) % 2 == 1
+        chosen = (away & bit) != 0
         gain = tuple(jnp.where(chosen, taken[k], gain[k]) for k in range(2))
         factor = complex_times(factor, factor)
         bit = bit * 2
     weight = jnp.sqrt(1.0 - back_decay * back_decay)
-    imaginary = lax.broadcasted_iota(jnp.int32, (count, state), 1) % 2 == 1
+    imaginary = (lax.broadcasted_iota(jnp.int32, (count, state), 1) & 1) == 1
     direct = gain[0] * weight
     crossed = jnp.where(imaginary, gain[1], -gain[1]) * weight
 
@@ -384,14 +399,7 @@
     partner = jnp.where(
         imaginary, pltpu.roll(drives, 1, 1), pltpu.roll(drives, state - 1, 1)
     )
-    smoothed = jnp.sum(direct * drives + crossed * partner, axis=0, keepdims=True)
-    out_ref[...] = lax.dot_general(
-        smoothed,
-        readout_ref[...],
-        (((1,), (1,)), ((), ())),
-        precision=lax.Precision.HIGHEST,
-        preferred_element_type=jnp.float32,
-    )
+    out_ref[...] = jnp.sum(direct * drives + crossed * partner, axis=0, keepdims=True)
 
     def sent(step, carry):
         copy_to(step).wait_send()
@@ -400,14 +408,14 @@
     lax.fori_loop(1, count, sent, 0)
 
 
-def filtered_latent(observed, input_map, modes, readout):
+def smoothed_state(observed, input_map, *modes):
     count = lax.axis_size("tm")
-    state = observed.shape[1]
+    state = input_map.shape[0]
     vmem = pl.BlockSpec(memory_space=pltpu.VMEM)
     return pl.pallas_call(
         functools.partial(filter_kernel, count),
-        out_shape=jax.ShapeDtypeStruct((1, readout.shape[0]), jnp.float32),
-        in_specs=[vmem] * 4,
+        out_shape=jax.ShapeDtypeStruct((1, state), jnp.float32),
+        in_specs=[vmem] * 6,
         out_specs=vmem,
         scratch_shapes=[
             pltpu.VMEM((count, 1, state), jnp.float32),
@@ -416,7 +424,7 @@
         ],
         compiler_params=pltpu.CompilerParams(collective_id=0, has_side_effects=True),
         name="filters",
-    )(observed, input_map, modes, readout)
+    )(observed, input_map, *(mode.reshape(1, -1) for mode in modes))
 
 
 def encode_tiles(frames, patch_weight, depth_weight, point_weight, observe_weight):
@@ -465,8 +473,10 @@
         observed = encode_tiles(movie_frames, *encoder)
         share = readout.shape[0] // tile_count
         readout = lax.dynamic_slice_in_dim(readout, lax.axis_index("tile") * share, share, 0)
-    modes = jnp.stack([mode_decay, mode_angle, smooth_decay, smooth_angle])
-    return filtered_latent(observed, input_map, modes, readout)
+    smoothed = smoothed_state(
+        observed, input_map, mode_decay, mode_angle, smooth_decay, smooth_angle
+    )
+    return jnp.dot(smoothed, readout.T, precision=lax.Precision.HIGHEST)
 
 
 def solution(mesh):

time: 55.6 us -> 53.5 us (0.962)
  local copies, waits for them, and re-layouts: 2.58 us -> 0.01 us
  matrix products: 0 us -> 1.55 us
  other arithmetic: 0.57 us -> 0 us
    dot_general x0 -> x1, matrix products: none -> 1.55 us  [shards(): return jnp.dot(smoothed, readout.T, precision=lax.Precision.HIGHEST)]
    reshape x1 -> x0, local copies, waits for them, and re-layouts: 1.36 us -> none  [encode_whole(): depth_weight.reshape(-1, channels)]
    unnamed x9 -> x2, local copies, waits for them, and re-layouts: 1.21 us -> 0.01 us
    another operation x1 -> x0, other arithmetic: 0.57 us -> none  [shards(): modes = jnp.stack([mode_decay, mode_angle, smooth_decay, smooth_angle])]
where the time goes in v6:
time: 53.5 us; the launch traced here: 53.3 us
  Pallas kernels  51.8 us (97%)
  matrix products  1.55 us (3%)
    pallas_call x1, Pallas kernels, encode_whole(): pl.pallas_call(encoder_kernel, out_shape=jax.ShapeDtypeStruct((1, compone...  40 us
    pallas_call x1, Pallas kernels, smoothed_state(): pl.pallas_call(functools.partial(filter_kernel, count), out_shape=jax.Sha...  11.7 us
    dot_general x1, matrix products, shards(): return jnp.dot(smoothed, readout.T, precision=lax.Precision.HIGHEST)  1.55 us

profile of v6, /device:TPU:0, one launch (start us, length us, event | category | flops | bytes accessed | tf_op | source)
XLA Modules:
  0.0 53.3 jit_solution(11617695389788419152)
XLA Ops:
  0.0 0.0 copy-start
  0.0 40.0 %encoder.1.observed_ref = f32[1,256]{1,0:T(1,128)} custom-call(bf16[1024,1024]{1,0:T(8,128)(2,1)} %bitcast.13, bf16[64,128]{1,0:T(8,128)(2,1)} %patch_ref.1, bf16[3,3,3,128]{3,2,1,0:T(4,128)(2,1)} %depth_ref.1, bf16[3,128,128]{2,1,0:T(8,128)(2,1)} %point_ref.1, bf16[16,2048,256]{2,1,0:T(8,128)(2,1)} %bitcast.12), custom_call_target="tpu_custom_call" | custom-call | tf_op jit(solution)/shard_map/encoder/pallas_call | solution.py:263
  40.0 11.7 %filters.1 = f32[1,256]{1,0:T(1,128)} custom-call(f32[1,256]{1,0:T(1,128)} %encoder.1.observed_ref, f32[256,256]{1,0:T(8,128)} %map_ref.1, f32[1,128]{1,0:T(1,128)} %bitcast.14, f32[1,128]{1,0:T(1,128)} %bitcast.15, f32[1,128]{1,0:T(1,128)} %bitcast.16, f32[1,128]{1,0:T(1,128)} %bitcast.17), custom_call_target="tpu_custom_call" | custom-call | tf_op jit(solution)/shard_map/filters/pallas_call | solution.py:415
  51.8 0.0 copy-done
  51.8 1.5 %fusion = f32[1,256]{1,0:T(1,128)} fusion(f32[256,256]{1,0:T(8,128)S(1)} %copy-done, f32[1,256]{1,0:T(1,128)} %filters.1), kind=kOutput, calls=%fused_computation | convolution fusion | flops 786432 | bytes 264192 | tf_op jit(solution)/shard_map/dot_general | solution.py:479
Async XLA Ops:
  0.0 51.8 %copy-start = (f32[256,256]{1,0:T(8,128)S(1)}, f32[256,256]{1,0:T(8,128)}, u32[]{:S(2)}) copy-start(f32[256,256]{1,0:T(8,128)} %param.21) | copy-start | bytes 786436
